TPU v7x, 32 devices: a whole 2x2x4 slice. The times are simulated.
32 devices in a mesh: batch: 8 (over z, x), seq: 4 (over y, core).
Axes of the slice: x: 2, y: 2, z: 4, core: 2. Of those that a mesh axis runs over, the one named last changes fastest.
Arguments:
- tokens: bfloat16 [24576, 768], P(('batch', 'seq')), may hold values from -6 to 6
- group_bucket: int32 [8], P('batch'), may hold values from 0 to 1, as said below
- lengths: int32 [8, 3], P('batch'), may hold values from 0 to 3072, as said below
- random_blocks: int32 [8, 48, 3], P('batch'), may hold values from 1 to 46, as said below
- w_qkv: bfloat16 [768, 2304], replicated, may hold values from -0.21875 to 0.21875
- w_out: bfloat16 [768, 768], replicated, may hold values from -1.25 to 1.25
- b_out: float32 [768], replicated, may hold values from -3 to 3
- norm1_gain: float32 [768], replicated, may hold values from 0.5 to 1.5
- norm1_shift: float32 [768], replicated, may hold values from -3 to 3
- w_in: bfloat16 [768, 3072], replicated, may hold values from -0.21875 to 0.21875
- b_in: float32 [3072], replicated, may hold values from -3 to 3
- w_back: bfloat16 [3072, 768], replicated, may hold values from -0.109375 to 0.109375
- b_back: float32 [768], replicated, may hold values from -3 to 3
- norm2_gain: float32 [768], replicated, may hold values from 0.5 to 1.5
- norm2_shift: float32 [768], replicated, may hold values from -3 to 3
- cotangent: bfloat16 [24576, 768], P(('batch', 'seq')), may hold values from -6 to 6
Outputs:
- layer_out: bfloat16 [24576, 768], P(('batch', 'seq'))
- grad_tokens: bfloat16 [24576, 768], P(('batch', 'seq'))
- grad_w_qkv: float32 [768, 2304], replicated
- grad_w_out: float32 [768, 768], replicated
- grad_b_out: float32 [768], replicated
- grad_norm1_gain: float32 [768], replicated
- grad_norm1_shift: float32 [768], replicated
- grad_w_in: float32 [768, 3072], replicated
- grad_b_in: float32 [3072], replicated
- grad_w_back: float32 [3072, 768], replicated
- grad_b_back: float32 [768], replicated
- grad_norm2_gain: float32 [768], replicated
- grad_norm2_shift: float32 [768], replicated
Inputs may be any that keep to these rules, and one draw needn't show every extreme that they name: `group_bucket`: both buckets occur among the groups. `lengths`: in a group of bucket 0 every entry exceeds 3 * 256 and is at most 1024, and some such sequence has exactly 1024; in a group of bucket 1 entry 0 exceeds 3 * 768, the other entries are 0, and some such group has exactly 3072. `random_blocks`: each entry is a block of the query block's own sequence that starts below that sequence's length, is neither the query block nor next to it nor the sequence's first or last block; the three entries of a query block differ.
All inputs are finite; a program needn't handle non-finite values.
Results may differ from a plain program's by a relative error of at most 0.014.
Values may be sent and summed in bfloat16 or wider, within the bound.
A program may use at most 192 MiB of HBM per device.

v0:
```python
import jax
import jax.numpy as jnp
from jax import lax
from jax.sharding import PartitionSpec as P

HEADS = 12
HEAD = 64
BLOCK = 64
SHORT = 1024


norm_eps = 1e-06
query_span = 8
listed_blocks = 8
masked_score = -1e30


def sequence_layout(nblocks, short_blocks, group_flag, seq_lengths):
    own_block = jnp.arange(nblocks, dtype=jnp.int32)
    is_long = group_flag > 0
    member = jnp.where(is_long, 0, own_block // short_blocks)
    start_block = jnp.where(is_long, 0, member * short_blocks)
    span_blocks = jnp.where(is_long, nblocks, short_blocks).astype(jnp.int32)
    seq_slots = jnp.arange(seq_lengths.shape[0], dtype=jnp.int32)
    valid_len = jnp.sum(
        jnp.where(member[:, None] == seq_slots[None, :], seq_lengths[None, :], 0), axis=1
    )
    return (own_block, start_block, span_blocks, valid_len)


def block_keys(nblocks, short_blocks, block_rows, group_flag, seq_lengths, random_ids):
    own_block, start_block, span_blocks, valid_len = sequence_layout(
        nblocks, short_blocks, group_flag, seq_lengths
    )
    end_block = start_block + span_blocks
    window = jnp.stack([own_block - 1, own_block, own_block + 1], axis=1)
    edge_blocks = jnp.stack([start_block, end_block - 1], axis=1)
    listed = jnp.concatenate([window, random_ids, edge_blocks], axis=1)
    inside = (listed >= start_block[:, None]) & (listed < end_block[:, None])
    column = jnp.arange(listed_blocks, dtype=jnp.int32)
    repeated = (column[None, :] >= 6) & (jnp.abs(listed - own_block[:, None]) <= 1)
    inside = inside & jnp.logical_not(repeated)
    places = (listed - start_block[:, None])[:, :, None] * block_rows + jnp.arange(
        block_rows, dtype=jnp.int32
    )[None, None, :]
    allowed = inside[:, :, None] & (places < valid_len[:, None, None])
    return (jnp.clip(listed, 0, nblocks - 1), allowed.reshape(nblocks, listed_blocks * block_rows))


def global_layout(nblocks, short_blocks, block_rows, group_flag, seq_lengths):
    seq_count = seq_lengths.shape[0]
    seq_slots = jnp.arange(seq_count, dtype=jnp.int32)
    is_long = group_flag > 0
    first_block = jnp.where(is_long, 0, seq_slots * short_blocks)
    last_block = jnp.where(is_long, nblocks - 1, seq_slots * short_blocks + short_blocks - 1)
    seq_valid = jnp.where(is_long, seq_lengths[0], seq_lengths)
    keep_seq = jnp.where(is_long, seq_slots == 0, True)
    global_ids = jnp.stack([first_block, last_block], axis=1).reshape(2 * seq_count)
    global_keep = jnp.repeat(keep_seq, 2).astype(jnp.float32)
    positions = jnp.arange(nblocks * block_rows, dtype=jnp.int32)
    offsets = positions[None, :] - first_block[:, None] * block_rows
    open_seq = (
        (offsets >= 0)
        & (positions[None, :] < (last_block[:, None] + 1) * block_rows)
        & (offsets < seq_valid[:, None])
    )
    open_rows = jnp.repeat(jnp.repeat(open_seq, 2, axis=0), block_rows, axis=0)
    return (global_ids, global_keep, open_rows)


def plain_dot(left, right):
    return jnp.dot(left, right, preferred_element_type=jnp.float32)


def left_dot(left, right):
    return lax.dot_general(
        left, right, (((0,), (0,)), ((), ())), preferred_element_type=jnp.float32
    )


def right_dot(left, right):
    return lax.dot_general(
        left, right, (((1,), (1,)), ((), ())), preferred_element_type=jnp.float32
    )


def normalize(values, norm_gain, norm_shift):
    centred = values - jnp.mean(values, axis=-1, keepdims=True)
    spread_inv = lax.rsqrt(jnp.mean(centred * centred, axis=-1, keepdims=True) + norm_eps)
    unit_value = centred * spread_inv
    return (unit_value * norm_gain + norm_shift, unit_value, spread_inv)


def normalize_back(grad_values, unit_value, spread_inv, norm_gain):
    scaled = grad_values * norm_gain
    centred = (
        scaled
        - jnp.mean(scaled, axis=-1, keepdims=True)
        - unit_value * jnp.mean(scaled * unit_value, axis=-1, keepdims=True)
    )
    return (
        spread_inv * centred,
        jnp.sum(grad_values * unit_value, axis=0),
        jnp.sum(grad_values, axis=0),
    )


def span_scores(span_queries, gathered_keys, span_allowed, factor):
    scores = (
        jnp.einsum(
            "hbqe,hbke->hbqk", span_queries, gathered_keys, preferred_element_type=jnp.float32
        )
        * factor
    )
    return jnp.where(span_allowed[None, :, None, :], scores, masked_score)


def gather_blocks(key_rows, value_rows, span_listed):
    head_group = key_rows.shape[0]
    gathered_keys = key_rows[:, span_listed].reshape(
        head_group, query_span, listed_blocks * BLOCK, HEAD
    )
    gathered_values = value_rows[:, span_listed].reshape(
        head_group, query_span, listed_blocks * BLOCK, HEAD
    )
    return (gathered_keys, gathered_values)


def span_slices(query_rows, listed, allowed, start):
    head_group = query_rows.shape[0]
    span_queries = lax.dynamic_slice_in_dim(query_rows, start, query_span, 1).reshape(
        head_group, query_span, BLOCK, HEAD
    )
    span_listed = lax.dynamic_slice_in_dim(listed, start, query_span, 0)
    span_allowed = lax.dynamic_slice_in_dim(allowed, start, query_span, 0)
    return (span_queries, span_listed, span_allowed)


def sparse_forward(query_rows, key_rows, value_rows, listed, allowed, factor):
    head_group, nblocks, width = query_rows.shape
    span_count = nblocks // query_span

    def one_span(index, carry):
        result_rows, totals = carry
        start = index * query_span
        span_queries, span_listed, span_allowed = span_slices(query_rows, listed, allowed, start)
        gathered_keys, gathered_values = gather_blocks(key_rows, value_rows, span_listed)
        scores = span_scores(span_queries, gathered_keys, span_allowed, factor)
        row_max = jnp.max(scores, axis=-1, keepdims=True)
        log_total = jnp.log(jnp.sum(jnp.exp(scores - row_max), axis=-1, keepdims=True)) + row_max
        weights = jnp.exp(scores - log_total).astype(jnp.bfloat16)
        result = jnp.einsum(
            "hbqk,hbke->hbqe", weights, gathered_values, preferred_element_type=jnp.float32
        )
        result_rows = lax.dynamic_update_slice_in_dim(
            result_rows, result.reshape(head_group, query_span, width), start, 1
        )
        totals = lax.dynamic_update_slice_in_dim(totals, log_total[..., 0], start, 1)
        return (result_rows, totals)

    initial = (
        jnp.zeros((head_group, nblocks, width), jnp.float32),
        jnp.zeros((head_group, nblocks, BLOCK), jnp.float32),
    )
    return lax.fori_loop(0, span_count, one_span, initial)


def sparse_back(query_rows, key_rows, value_rows, grad_rows, listed, allowed, totals, factor):
    head_group, nblocks, width = query_rows.shape
    span_count = nblocks // query_span

    def one_span(index, carry):
        query_grad, key_grad, value_grad = carry
        start = index * query_span
        span_queries, span_listed, span_allowed = span_slices(query_rows, listed, allowed, start)
        span_grads = lax.dynamic_slice_in_dim(grad_rows, start, query_span, 1).reshape(
            head_group, query_span, BLOCK, HEAD
        )
        log_total = lax.dynamic_slice_in_dim(totals, start, query_span, 1)[..., None]
        gathered_keys, gathered_values = gather_blocks(key_rows, value_rows, span_listed)
        scores = span_scores(span_queries, gathered_keys, span_allowed, factor)
        probability = jnp.exp(scores - log_total)
        weights = probability.astype(jnp.bfloat16)
        grad_weights = jnp.einsum(
            "hbqe,hbke->hbqk", span_grads, gathered_values, preferred_element_type=jnp.float32
        )
        centred = grad_weights - jnp.sum(probability * grad_weights, axis=-1, keepdims=True)
        grad_scores = (probability * centred).astype(jnp.bfloat16)
        span_query_grad = (
            jnp.einsum(
                "hbqk,hbke->hbqe", grad_scores, gathered_keys, preferred_element_type=jnp.float32
            )
            * factor
        )
        gathered_key_grad = (
            jnp.einsum(
                "hbqk,hbqe->hbke", grad_scores, span_queries, preferred_element_type=jnp.float32
            )
            * factor
        )
        gathered_value_grad = jnp.einsum(
            "hbqk,hbqe->hbke", weights, span_grads, preferred_element_type=jnp.float32
        )
        query_grad = lax.dynamic_update_slice_in_dim(
            query_grad, span_query_grad.reshape(head_group, query_span, width), start, 1
        )
        key_grad = key_grad.at[:, span_listed].add(
            gathered_key_grad.reshape(head_group, query_span, listed_blocks, width)
        )
        value_grad = value_grad.at[:, span_listed].add(
            gathered_value_grad.reshape(head_group, query_span, listed_blocks, width)
        )
        return (query_grad, key_grad, value_grad)

    zero_grads = jnp.zeros((head_group, nblocks, width), jnp.float32)
    return lax.fori_loop(0, span_count, one_span, (zero_grads, zero_grads, zero_grads))


def global_scores(global_queries, keys_all, open_rows, factor):
    scores = (
        jnp.einsum("hqe,hke->hqk", global_queries, keys_all, preferred_element_type=jnp.float32)
        * factor
    )
    return jnp.where(open_rows[None, :, :], scores, masked_score)


def global_forward(global_queries, keys_all, values_all, open_rows, factor):
    scores = global_scores(global_queries, keys_all, open_rows, factor)
    row_max = jnp.max(scores, axis=-1, keepdims=True)
    log_total = jnp.log(jnp.sum(jnp.exp(scores - row_max), axis=-1, keepdims=True)) + row_max
    weights = jnp.exp(scores - log_total).astype(jnp.bfloat16)
    return (
        jnp.einsum("hqk,hke->hqe", weights, values_all, preferred_element_type=jnp.float32),
        log_total,
    )


def global_back(global_queries, keys_all, values_all, global_grads, open_rows, log_total, factor):
    scores = global_scores(global_queries, keys_all, open_rows, factor)
    probability = jnp.exp(scores - log_total)
    weights = probability.astype(jnp.bfloat16)
    grad_weights = jnp.einsum(
        "hqe,hke->hqk", global_grads, values_all, preferred_element_type=jnp.float32
    )
    grad_scores = (
        probability * (grad_weights - jnp.sum(probability * grad_weights, axis=-1, keepdims=True))
    ).astype(jnp.bfloat16)
    query_grad = (
        jnp.einsum("hqk,hke->hqe", grad_scores, keys_all, preferred_element_type=jnp.float32)
        * factor
    )
    key_grad = (
        jnp.einsum("hqk,hqe->hke", grad_scores, global_queries, preferred_element_type=jnp.float32)
        * factor
    )
    value_grad = jnp.einsum(
        "hqk,hqe->hke", weights, global_grads, preferred_element_type=jnp.float32
    )
    return (query_grad, key_grad, value_grad)


def per_device(
    tokens,
    group_bucket,
    lengths,
    random_blocks,
    w_qkv,
    w_out,
    b_out,
    norm1_gain,
    norm1_shift,
    w_in,
    b_in,
    w_back,
    b_back,
    norm2_gain,
    norm2_shift,
    cotangent,
):
    seq_parts = lax.axis_size("seq")
    tok_rows, feat_width = tokens.shape
    head_group = HEADS // seq_parts
    seq_length = tok_rows * seq_parts
    nblocks = seq_length // BLOCK
    short_blocks = SHORT // BLOCK
    width = BLOCK * HEAD
    factor = HEAD ** (-0.5)
    group_flag = group_bucket[0]
    seq_lengths = lengths[0]
    seq_count = seq_lengths.shape[0]
    listed, allowed = block_keys(
        nblocks, short_blocks, BLOCK, group_flag, seq_lengths, random_blocks[0]
    )
    global_ids, global_keep, open_rows = global_layout(
        nblocks, short_blocks, BLOCK, group_flag, seq_lengths
    )
    is_global = jnp.any(
        jnp.arange(nblocks, dtype=jnp.int32)[:, None] == global_ids[None, :], axis=1
    )
    inputs = tokens.astype(jnp.float32)
    projected = plain_dot(tokens, w_qkv).astype(jnp.bfloat16)
    by_heads = lax.all_to_all(
        projected.reshape(tok_rows, 3, seq_parts, head_group * HEAD),
        "seq",
        split_axis=2,
        concat_axis=0,
        tiled=True,
    )
    head_major = by_heads.reshape(seq_length, 3, head_group, HEAD).transpose(1, 2, 0, 3)
    queries_all = head_major[0]
    keys_all = head_major[1]
    values_all = head_major[2]
    query_rows = queries_all.reshape(head_group, nblocks, width)
    key_rows = keys_all.reshape(head_group, nblocks, width)
    value_rows = values_all.reshape(head_group, nblocks, width)
    sparse_out, sparse_totals = sparse_forward(
        query_rows, key_rows, value_rows, listed, allowed, factor
    )
    global_queries = query_rows[:, global_ids].reshape(head_group, 2 * seq_count * BLOCK, HEAD)
    global_out, global_total = global_forward(
        global_queries, keys_all, values_all, open_rows, factor
    )
    global_placed = (
        global_out.reshape(head_group, 2 * seq_count, width) * global_keep[None, :, None]
    )
    placed = jnp.zeros(sparse_out.shape, jnp.float32).at[:, global_ids].add(global_placed)
    attention = jnp.where(is_global[None, :, None], placed, sparse_out)
    attention_low = (
        attention.astype(jnp.bfloat16).reshape(head_group, seq_length, HEAD).transpose(1, 0, 2)
    )
    attention_low = attention_low.reshape(seq_length, 1, head_group * HEAD)
    returned = lax.all_to_all(
        attention_low, "seq", split_axis=0, concat_axis=1, tiled=True
    ).reshape(tok_rows, feat_width)
    branch = plain_dot(returned, w_out) + b_out
    hidden, unit_first, spread_first = normalize(inputs + branch, norm1_gain, norm1_shift)
    hidden_low = hidden.astype(jnp.bfloat16)
    inner_pre = plain_dot(hidden_low, w_in) + b_in
    active, gelu_pull = jax.vjp(lambda value: jax.nn.gelu(value, approximate=False), inner_pre)
    active_low = active.astype(jnp.bfloat16)
    second = plain_dot(active_low, w_back) + b_back
    layer_out, unit_second, spread_second = normalize(hidden + second, norm2_gain, norm2_shift)
    grad_pre2, grad_gain2, grad_shift2 = normalize_back(
        cotangent.astype(jnp.float32), unit_second, spread_second, norm2_gain
    )
    grad_second = grad_pre2.astype(jnp.bfloat16)
    grad_w_back = left_dot(active_low, grad_second)
    grad_b_back = jnp.sum(grad_second.astype(jnp.float32), axis=0)
    grad_inner = gelu_pull(right_dot(grad_second, w_back))[0].astype(jnp.bfloat16)
    grad_w_in = left_dot(hidden_low, grad_inner)
    grad_b_in = jnp.sum(grad_inner.astype(jnp.float32), axis=0)
    grad_hidden = grad_pre2 + right_dot(grad_inner, w_in)
    grad_pre1, grad_gain1, grad_shift1 = normalize_back(
        grad_hidden, unit_first, spread_first, norm1_gain
    )
    grad_branch = grad_pre1.astype(jnp.bfloat16)
    grad_w_out = left_dot(returned, grad_branch)
    grad_b_out = jnp.sum(grad_branch.astype(jnp.float32), axis=0)
    grad_attention = right_dot(grad_branch, w_out).astype(jnp.bfloat16)
    grad_heads = lax.all_to_all(
        grad_attention.reshape(tok_rows, seq_parts, head_group * HEAD),
        "seq",
        split_axis=1,
        concat_axis=0,
        tiled=True,
    )
    grad_rows = (
        grad_heads.reshape(seq_length, head_group, HEAD)
        .transpose(1, 0, 2)
        .reshape(head_group, nblocks, width)
    )
    sparse_grads = jnp.where(is_global[None, :, None], jnp.zeros_like(grad_rows), grad_rows)
    query_grad, key_grad, value_grad = sparse_back(
        query_rows, key_rows, value_rows, sparse_grads, listed, allowed, sparse_totals, factor
    )
    global_grads = grad_rows[:, global_ids] * global_keep.astype(jnp.bfloat16)[None, :, None]
    global_grads = global_grads.reshape(head_group, 2 * seq_count * BLOCK, HEAD)
    global_query_grad, global_key_grad, global_value_grad = global_back(
        global_queries, keys_all, values_all, global_grads, open_rows, global_total, factor
    )
    query_grad = query_grad.at[:, global_ids].add(
        global_query_grad.reshape(head_group, 2 * seq_count, width)
    )
    key_grad = key_grad.reshape(head_group, seq_length, HEAD) + global_key_grad
    value_grad = value_grad.reshape(head_group, seq_length, HEAD) + global_value_grad
    stacked = jnp.stack(
        [query_grad.reshape(head_group, seq_length, HEAD), key_grad, value_grad], axis=0
    ).astype(jnp.bfloat16)
    stacked = stacked.transpose(2, 0, 1, 3).reshape(seq_length, 3, 1, head_group * HEAD)
    grad_projected = lax.all_to_all(
        stacked, "seq", split_axis=0, concat_axis=2, tiled=True
    ).reshape(tok_rows, 3 * feat_width)
    grad_w_qkv = left_dot(tokens, grad_projected)
    grad_tokens = (grad_pre1 + right_dot(grad_projected, w_qkv)).astype(jnp.bfloat16)
    summed = lax.psum(
        (
            grad_w_qkv,
            grad_w_out,
            grad_b_out,
            grad_gain1,
            grad_shift1,
            grad_w_in,
            grad_b_in,
            grad_w_back,
            grad_b_back,
            grad_gain2,
            grad_shift2,
        ),
        ("batch", "seq"),
    )
    return (
        layer_out.astype(jnp.bfloat16),
        grad_tokens,
        summed[0],
        summed[1],
        summed[2],
        summed[3],
        summed[4],
        summed[5],
        summed[6],
        summed[7],
        summed[8],
        summed[9],
        summed[10],
    )


def solution(mesh):
    placed = (
        P(("batch", "seq"), None),
        P("batch"),
        P("batch", None),
        P("batch", None, None),
        P(),
        P(),
        P(),
        P(),
        P(),
        P(),
        P(),
        P(),
        P(),
        P(),
        P(),
        P(("batch", "seq"), None),
    )
    return jax.shard_map(
        per_device,
        mesh=mesh,
        in_specs=placed,
        out_specs=(
            P(("batch", "seq"), None),
            P(("batch", "seq"), None),
            P(),
            P(),
            P(),
            P(),
            P(),
            P(),
            P(),
            P(),
            P(),
            P(),
            P(),
        ),
        check_vma=False,
    )
```

profile of v0, /device:TPU:25, one launch (start us, length us, event | category | flops | bytes accessed | tf_op | source)
XLA Modules:
  0.0 2037.4 jit_solution(625253019410993644)
XLA Ops:
  54.8 15.9 all-to-all-done
  122.6 266.5 %while.32 = (s32[]{:T(128)}, bf16[3,48,4096]{2,1,0:T(8,128)(2,1)}, f32[3,48,64]{2,1,0:T(8,128)}, pred[48,512]{1,0:T(8,128)(4,1)}, bf16[3,48,4096]{2,1,0:T(8,128)...) while((s32[]{:T(128)}, bf16[3,48,4096]{2,1,0:T(8,128)(2,1)}, ...), condition=%wide.region_8.9_spmd, body=%wide.region_5.8_spmd.sunk | while | flops 209977024 | bytes 39796696 | solution.py:165
  499.9 30.6 %multiply_convert_fusion.2 = (bf16[768,3072]{1,0:T(8,128)(2,1)S(1)}, f32[768,3072]{1,0:T(8,128)}, f32[768,3072]{1,0:T(8,128)}) fusion(f32[3072]{0:T(1024)S(1)} %copy-done.49, bf16[768,3072]{1,0:T(8,128)(2,1)} %param.29, f32[768,768]{0,1:T(8,128)S(1)} %get-tuple-element.618, f32[768]{0:T(1024)S(1)} %copy-done.52, f32[768]{0:T(1024)S(1)} %copy-done.43, ...), kind=kOutput, calls=%fused_computation.56 | convolution fusion | flops 3782541312 | bytes 30695424 | tf_op jit(solution)/shard_map/dot_general | solution.py:72
  540.9 13.2 convert_reduce_fusion
  574.2 14.3 all-to-all-done.2
  614.5 749.2 %while.33 = (s32[]{:T(128)}, f32[3,48,4096]{2,1,0:T(8,128)}, f32[3,48,4096]{2,0,1:T(4,128)}, f32[3,48,4096]{2,0,1:T(4,128)}, pred[48,512]{1,0:T(8,128)(4,1)}, /*...) while((s32[]{:T(128)}, f32[3,48,4096]{2,1,0:T(8,128)}, ...), condition=%wide.region_21.22_spmd, body=%wide.region_17.21_spmd.sunk | while | flops 512851648 | bytes 145949296 | solution.py:216
  691.7 15.2 scatter_fusion
  724.5 15.2 scatter_fusion.1
  816.5 15.2 scatter_fusion
  849.3 15.2 scatter_fusion.1
  941.3 15.2 scatter_fusion
  974.1 15.2 scatter_fusion.1
  1066.0 15.2 scatter_fusion
  1098.8 15.2 scatter_fusion.1
  1190.8 15.2 scatter_fusion
  1223.6 15.2 scatter_fusion.1
  1315.6 15.2 scatter_fusion
  1348.3 15.2 scatter_fusion.1
  1387.1 11.2 multiply_reduce_fusion.1
  1421.9 11.0 multiply_convert_fusion.1
  1504.2 49.6 %all-to-all-done.3 = bf16[3072,3,1,192]{3,1,2,0:T(4,128)(2,1)} async-done(((bf16[3072,3,1,192]{3,1,2,0:T(4,128)(2,1)}), bf16[3072,3,1,192]{3,1,2,0:T(4,128)(2,1)}, u32[]{:S(2)}, u32[]{:S(2)}) %all-to-all-start.3) | async-done | bytes 3538976 | tf_op jit(solution)/shard_map/all_to_all | solution.py:390
  1553.8 10.5 copy.394
  1576.1 41.6 %all-reduce = (f32[768]{0:T(1024)}, f32[768]{0:T(1024)}, f32[768]{0:T(1024)}, f32[3072]{0:T(1024)}, f32[768]{0:T(1024)}, /*index=5*/f32[768]{0:T(1024)}, f32[768]{0:T(1024)}) all-reduce(f32[768]{0:T(1024)S(1)} %copy-done.31, f32[768]{0:T(1024)} %get-tuple-element.536, ...), channel_id=1, replica_groups=mesh['batch'=8,'seq'=4] {'batch','seq'}, use_global_device_ids=true, to_apply=%region_27.28 | all-reduce | flops 7680 | bytes 61440 | tf_op jit(solution)/shard_map/psum | solution.py:395
  1626.7 379.5 %all-reduce.4.cloned.1.call-done = (f32[768,2304]{0,1:T(8,128)}, f32[768,768]{1,0:T(8,128)}, f32[768,3072]{1,0:T(8,128)}, f32[3072,768]{1,0:T(8,128)}) async-done(((f32[768,2304]{0,1:T(8,128)}, f32[768,768]{1,0:T(8,128)}, f32[768,3072]{1,0:T(8,128)}, f32[3072,768]{1,0:T(8,128)}), (f32[768,2304]{0,1:T(8,128)}, f32[768,768]{1,0:T(8,128)}, f32[768,3072]{1,0:T(8,128)}, ...) | async-done | bytes 28311568 | tf_op jit(solution)/shard_map/psum | solution.py:395
  (607 shorter events, 1260.2 us)
Async XLA Ops:
  24.8 45.9 %all-to-all-start = ((bf16[768,3,4,192]{0,3,1,2:T(8,128)(2,1)}), bf16[768,3,4,192]{0,3,1,2:T(8,128)(2,1)}, u32[]{:S(2)}, u32[]{:S(2)}) async-start(bf16[768,3,4,192]{0,3,1,2:T(8,128)(2,1)} %copy.330), calls=%async_computation | async-start | bytes 7077888 | tf_op jit(solution)/shard_map/all_to_all | solution.py:302
  50.0 339.1 %copy-start.38 = (s32[1024]{0:T(1024)}, s32[1024]{0:T(1024)S(1)}, u32[]{:S(2)}) copy-start(s32[1024]{0:T(1024)S(1)} %pad_clamp_fusion.2) | copy-start | bytes 12292
  396.7 18.7 copy-start.7
  416.0 11.6 copy-start.46
  459.0 20.2 all-to-all-start.1
  496.1 34.4 %slice-start.3 = ((s8[4718592]{0:T(1024)(128)(4,1)}), s8[4194304]{0:T(1024)(128)(4,1)S(1)}, s32[]{:S(2)}) async-start(s8[4718592]{0:T(1024)(128)(4,1)} %bitcast.229), calls=%async_computation.8 | async-start | bytes 8388608
  499.5 63.8 %copy-start.13 = (f32[768,768]{0,1:T(8,128)}, f32[768,768]{0,1:T(8,128)S(1)}, u32[]{:S(2)}) copy-start(f32[768,768]{0,1:T(8,128)S(1)} %get-tuple-element.618) | copy-start | bytes 7077892
  499.5 63.8 %copy-start.28 = (f32[768]{0:T(1024)}, f32[768]{0:T(1024)S(1)}, u32[]{:S(2)}) copy-start(f32[768]{0:T(1024)S(1)} %broadcast_multiply_fusion.5) | copy-start | bytes 9220
  499.8 63.4 %copy-start.32 = (f32[768]{0:T(1024)}, f32[768]{0:T(1024)S(1)}, u32[]{:S(2)}) copy-start(f32[768]{0:T(1024)S(1)} %add_rsqrt_fusion.1) | copy-start | bytes 9220
  499.8 30.6 %slice-start.4 = ((s8[4718592]{0:T(1024)(128)(4,1)}), s8[524288]{0:T(1024)(128)(4,1)S(1)}, s32[]{:S(2)}) async-start(s8[4718592]{0:T(1024)(128)(4,1)} %bitcast.229), calls=%async_computation.9 | async-start | bytes 1048576
  499.9 30.6 %copy-start.51 = (f32[768]{0:T(1024)S(1)}, f32[768]{0:T(1024)}, u32[]{:S(2)}) copy-start(f32[768]{0:T(1024)} %param.32) | copy-start | bytes 9220
  540.9 13.2 copy-start.21
  568.4 20.2 all-to-all-start.2
  1373.6 13.6 copy-start.27
  1387.1 11.2 copy-start.8
  1387.1 11.2 copy-start.19
  1387.1 11.3 copy-start.25
  1387.1 11.3 copy-start.37
  1398.4 10.4 copy-start.5
  1439.8 9.3 copy-start.41
  1477.9 76.0 %all-to-all-start.3 = ((bf16[3072,3,1,192]{3,1,2,0:T(4,128)(2,1)}), bf16[3072,3,1,192]{3,1,2,0:T(4,128)(2,1)}, u32[]{:S(2)}, u32[]{:S(2)}) async-start(bf16[3072,3,1,192]{3,1,2,0:T(4,128)(2,1)} %copy.373), calls=%async_computation.3 | async-start | bytes 12582912 | tf_op jit(solution)/shard_map/all_to_all | solution.py:390
  1483.9 522.3 %all-reduce.4.cloned.1.call-start = ((), (), s32[]{:S(2)}) async-start(), calls=%async_computation.4 | async-start | bytes 56623104 | tf_op jit(solution)/shard_map/psum | solution.py:395
  1483.9 13.7 slice-start.5
  2014.2 12.1 slice-start
  (73 other events, 303.8 us)
Sparse Core Ops, SparseCore 0:
  1573.8 432.3 all-reduce.3
where the time goes:
time: 2060 us; the launch traced here: 2040 us
  local copies, waits for them, and re-layouts  927 us (45%)
  waiting for transfers between devices  470 us (23%)
  matrix products  300 us (15%)
  other arithmetic  261 us (13%)
  blocking collectives  41.6 us (2%)
  starting transfers between devices  21.8 us (1%)
    psum x1, waiting for transfers between devices, per_device(): lax.psum((grad_w_qkv, grad_w_out, grad_b_out, grad_gain1, grad_shift1, gr...  380 us
    gather x24, local copies, waits for them, and re-layouts, gather_blocks(): key_rows[:, span_listed]  107 us
    gather x24, local copies, waits for them, and re-layouts, gather_blocks(): value_rows[:, span_listed]  106 us
    scatter-add x6, other arithmetic, one_span(): key_grad.at[:, span_listed]  91.1 us
    scatter-add x6, other arithmetic, one_span(): value_grad.at[:, span_listed]  91.1 us
    reshape x12, local copies, waits for them, and re-layouts, one_span(): gathered_value_grad.reshape(head_group, query_span, listed_blocks, width)  71.5 us
    reshape x12, local copies, waits for them, and re-layouts, one_span(): gathered_key_grad.reshape(head_group, query_span, listed_blocks, width)  71.4 us
    reshape x12, local copies, waits for them, and re-layouts, gather_blocks(): value_rows[:, span_listed]  65.9 us
  transfers between devices with their start and end apart: 5, of which 5 were waited for; matrix products, arithmetic and copies ran while one was open for 3% of the time, Pallas kernels for 0%

commit v1 on v0

v1 whole, which is shorter than its diff:
```python
import functools
import jax
import jax.numpy as jnp
from jax import lax
from jax.sharding import PartitionSpec as P
from jax.experimental import pallas as pl
from jax.experimental.pallas import tpu as pltpu

HEADS = 12
HEAD = 64
BLOCK = 64
SHORT = 1024
LISTED = 8
QUAD = 4
WIDE = QUAD * HEAD
SPAN = LISTED * BLOCK
MASKED = -1e30
NORM_EPS = 1e-06
NT = (((1,), (1,)), ((), ()))
TN = (((0,), (0,)), ((), ()))


def dot(a, b, dims=(((1,), (0,)), ((), ()))):
    return lax.dot_general(a, b, dims, preferred_element_type=jnp.float32)


def stack_heads(rows, head_mask):
    return jnp.concatenate([rows] * QUAD, axis=0) * head_mask


def pick_heads(full, lane_head):
    out = full[0:BLOCK]
    for h in range(1, QUAD):
        out = jnp.where(lane_head == h, full[h * BLOCK : (h + 1) * BLOCK], out)
    return out


def masked_span(scores, row_id, limits):
    parts = []
    for j in range(LISTED):
        parts.append(
            jnp.where(row_id < limits[j], scores[j * BLOCK : (j + 1) * BLOCK], MASKED)
        )
    return jnp.concatenate(parts, axis=0)


def attend_kernel(
    blocks, ids_ref, lim_ref, glob_ref, q_ref, k_ref, v_ref, hm_ref, o_ref, l_ref, kcat, vcat, acc
):
    row_id = lax.broadcasted_iota(jnp.int32, (BLOCK, WIDE), 0)
    lane_head = lax.broadcasted_iota(jnp.int32, (BLOCK, WIDE), 1) // HEAD
    chunk_row = lax.broadcasted_iota(jnp.int32, (SPAN, WIDE), 0)

    def one_block(b, carry):
        rows = pl.ds(pl.multiple_of(b * BLOCK, BLOCK), BLOCK)
        qm = stack_heads(q_ref[rows, :], hm_ref[...])
        for j in range(LISTED):
            src = pl.ds(pl.multiple_of(ids_ref[b * LISTED + j] * BLOCK, BLOCK), BLOCK)
            kcat[j * BLOCK : (j + 1) * BLOCK, :] = k_ref[src, :]
            vcat[j * BLOCK : (j + 1) * BLOCK, :] = v_ref[src, :]
        limits = [lim_ref[b * LISTED + j] for j in range(LISTED)]
        scores = masked_span(dot(kcat[...], qm, NT), row_id, limits)
        top = jnp.max(scores, axis=0, keepdims=True)
        grown = jnp.exp(scores - top)
        total = jnp.sum(grown, axis=0, keepdims=True)
        weights = (grown * (1.0 / total)).astype(jnp.bfloat16)
        full = dot(weights, vcat[...], TN)
        o_ref[rows, :] = pick_heads(full, lane_head).astype(jnp.bfloat16)
        l_ref[0, pl.ds(b, 1), :] = top + jnp.log(total)
        return carry

    lax.fori_loop(0, blocks, one_block, 0, unroll=UNROLL_F)

    def one_global(b, carry):
        @pl.when(glob_ref[b * 4] > 0)
        def _():
            rows = pl.ds(pl.multiple_of(b * BLOCK, BLOCK), BLOCK)
            qm = stack_heads(q_ref[rows, :], hm_ref[...])
            first = glob_ref[b * 4 + 1]
            valid = glob_ref[b * 4 + 3]
            acc[...] = jnp.zeros_like(acc)

            def one_chunk(c, state):
                top, total = state
                src = pl.ds(pl.multiple_of(first + c * SPAN, BLOCK), SPAN)
                scores = dot(k_ref[src, :], qm, NT)
                scores = jnp.where(chunk_row < valid - c * SPAN, scores, MASKED)
                newer = jnp.maximum(top, jnp.max(scores, axis=0, keepdims=True))
                shrink = jnp.exp(top - newer)
                grown = jnp.exp(scores - newer)
                acc[...] = acc[...] * shrink + dot(v_ref[src, :], grown.astype(jnp.bfloat16), TN)
                return (newer, total * shrink + jnp.sum(grown, axis=0, keepdims=True))

            top, total = lax.fori_loop(
                0,
                glob_ref[b * 4 + 2],
                one_chunk,
                (jnp.full((1, WIDE), MASKED, jnp.float32), jnp.zeros((1, WIDE), jnp.float32)),
            )
            full = (acc[...] * (1.0 / total)).T
            o_ref[rows, :] = pick_heads(full, lane_head).astype(jnp.bfloat16)
            l_ref[0, pl.ds(b, 1), :] = top + jnp.log(total)

        return carry

    lax.fori_loop(0, blocks, one_global, 0)

UNROLL_F = 2
UNROLL_B = 2

def smem():
    return pl.BlockSpec(memory_space=pltpu.SMEM)


def attend(ids, limits, glob, queries, kv, head_mask):
    rows, feat = queries.shape
    keys = kv.shape[0]
    quads = feat // WIDE
    blocks = rows // BLOCK
    pad_blocks = -(-blocks // 8) * 8
    return pl.pallas_call(
        functools.partial(attend_kernel, blocks),
        grid=(quads,),
        out_shape=(
            jax.ShapeDtypeStruct((rows, feat), jnp.bfloat16),
            jax.ShapeDtypeStruct((quads, pad_blocks, WIDE), jnp.float32),
        ),
        in_specs=[
            smem(),
            smem(),
            smem(),
            pl.BlockSpec((rows, WIDE), lambda i: (0, i)),
            pl.BlockSpec((keys, WIDE), lambda i: (0, i)),
            pl.BlockSpec((keys, WIDE), lambda i: (0, i + quads)),
            pl.BlockSpec((WIDE, WIDE), lambda i: (0, 0)),
        ],
        out_specs=[
            pl.BlockSpec((rows, WIDE), lambda i: (0, i)),
            pl.BlockSpec((1, pad_blocks, WIDE), lambda i: (i, 0, 0)),
        ],
        scratch_shapes=[
            pltpu.VMEM((SPAN, WIDE), jnp.bfloat16),
            pltpu.VMEM((SPAN, WIDE), jnp.bfloat16),
            pltpu.VMEM((WIDE, WIDE), jnp.float32),
        ],
        compiler_params=pltpu.CompilerParams(vmem_limit_bytes=56 * 2**20),
        name="attend",
    )(ids, limits, glob, queries, kv, kv, head_mask)


def attend_back_kernel(
    blocks, ids_ref, lim_ref, glob_ref, q_ref, k_ref, v_ref, g_ref, o_ref, l_ref, hm_ref,
    dq_ref, dk_ref, dv_ref, kcat, vcat, dk_sum, dv_sum, acc,
):
    row_id = lax.broadcasted_iota(jnp.int32, (BLOCK, WIDE), 0)
    lane_head = lax.broadcasted_iota(jnp.int32, (BLOCK, WIDE), 1) // HEAD
    chunk_row = lax.broadcasted_iota(jnp.int32, (SPAN, WIDE), 0)
    dk_sum[...] = jnp.zeros_like(dk_sum)
    dv_sum[...] = jnp.zeros_like(dv_sum)
    factor = HEAD ** (-0.5)

    def one_block(b, carry):
        rows = pl.ds(pl.multiple_of(b * BLOCK, BLOCK), BLOCK)
        keep = jnp.where(glob_ref[b * 4] > 0, 0.0, 1.0).astype(jnp.bfloat16)
        qm = stack_heads(q_ref[rows, :], hm_ref[...])
        gm = stack_heads(g_ref[rows, :] * keep, hm_ref[...])
        starts = [pl.multiple_of(ids_ref[b * LISTED + j] * BLOCK, BLOCK) for j in range(LISTED)]
        for j in range(LISTED):
            kcat[j * BLOCK : (j + 1) * BLOCK, :] = k_ref[pl.ds(starts[j], BLOCK), :]
            vcat[j * BLOCK : (j + 1) * BLOCK, :] = v_ref[pl.ds(starts[j], BLOCK), :]
        limits = [lim_ref[b * LISTED + j] for j in range(LISTED)]
        scores = masked_span(dot(kcat[...], qm, NT), row_id, limits)
        chance = jnp.exp(scores - l_ref[0, pl.ds(b, 1), :])
        grad_w = dot(vcat[...], gm, NT)
        mean = jnp.sum(chance * grad_w, axis=0, keepdims=True)
        grad_s = (chance * (grad_w - mean)).astype(jnp.bfloat16)
        dk_part = dot(grad_s, qm)
        dv_part = dot(chance.astype(jnp.bfloat16), gm)
        for j in range(LISTED):
            dst = pl.ds(starts[j], BLOCK)
            dk_sum[dst, :] += dk_part[j * BLOCK : (j + 1) * BLOCK]
            dv_sum[dst, :] += dv_part[j * BLOCK : (j + 1) * BLOCK]
        full = dot(grad_s, kcat[...], TN)
        dq_ref[rows, :] = (pick_heads(full, lane_head) * factor).astype(jnp.bfloat16)
        return carry

    lax.fori_loop(0, blocks, one_block, 0, unroll=UNROLL_B)

    def one_global(b, carry):
        @pl.when(glob_ref[b * 4] > 0)
        def _():
            rows = pl.ds(pl.multiple_of(b * BLOCK, BLOCK), BLOCK)
            qm = stack_heads(q_ref[rows, :], hm_ref[...])
            gm = stack_heads(g_ref[rows, :], hm_ref[...])
            first = glob_ref[b * 4 + 1]
            valid = glob_ref[b * 4 + 3]
            log_total = l_ref[0, pl.ds(b, 1), :]
            both = (g_ref[rows, :].astype(jnp.float32) * o_ref[rows, :].astype(jnp.float32)).T
            mean = jnp.concatenate(
                [
                    jnp.sum(both[h * HEAD : (h + 1) * HEAD], axis=0, keepdims=True)
                    for h in range(QUAD)
                ],
                axis=1,
            )
            acc[...] = jnp.zeros_like(acc)

            def one_chunk(c, carry):
                src = pl.ds(pl.multiple_of(first + c * SPAN, BLOCK), SPAN)
                scores = dot(k_ref[src, :], qm, NT)
                scores = jnp.where(chunk_row < valid - c * SPAN, scores, MASKED)
                chance = jnp.exp(scores - log_total)
                grad_w = dot(v_ref[src, :], gm, NT)
                grad_s = (chance * (grad_w - mean)).astype(jnp.bfloat16)
                dk_sum[src, :] += dot(grad_s, qm)
                dv_sum[src, :] += dot(chance.astype(jnp.bfloat16), gm)
                acc[...] += dot(grad_s, k_ref[src, :], TN)
                return carry

            lax.fori_loop(0, glob_ref[b * 4 + 2], one_chunk, 0)
            dq_ref[rows, :] = (pick_heads(acc[...], lane_head) * factor).astype(jnp.bfloat16)

        return carry

    lax.fori_loop(0, blocks, one_global, 0)
    dk_ref[...] = dk_sum[...].astype(jnp.bfloat16)
    dv_ref[...] = dv_sum[...].astype(jnp.bfloat16)


def attend_back(ids, limits, glob, queries, kv, grads, mixed, logs, head_mask):
    rows, feat = queries.shape
    keys = kv.shape[0]
    quads = feat // WIDE
    blocks = rows // BLOCK
    pad_blocks = logs.shape[1]
    row_spec = pl.BlockSpec((rows, WIDE), lambda i: (0, i))
    key_spec = pl.BlockSpec((keys, WIDE), lambda i: (0, i))
    return pl.pallas_call(
        functools.partial(attend_back_kernel, blocks),
        grid=(quads,),
        out_shape=(
            jax.ShapeDtypeStruct((rows, feat), jnp.bfloat16),
            jax.ShapeDtypeStruct((keys, feat), jnp.bfloat16),
            jax.ShapeDtypeStruct((keys, feat), jnp.bfloat16),
        ),
        in_specs=[
            smem(),
            smem(),
            smem(),
            row_spec,
            key_spec,
            pl.BlockSpec((keys, WIDE), lambda i: (0, i + quads)),
            row_spec,
            row_spec,
            pl.BlockSpec((1, pad_blocks, WIDE), lambda i: (i, 0, 0)),
            pl.BlockSpec((WIDE, WIDE), lambda i: (0, 0)),
        ],
        out_specs=[row_spec, key_spec, key_spec],
        scratch_shapes=[
            pltpu.VMEM((SPAN, WIDE), jnp.bfloat16),
            pltpu.VMEM((SPAN, WIDE), jnp.bfloat16),
            pltpu.VMEM((keys, WIDE), jnp.float32),
            pltpu.VMEM((keys, WIDE), jnp.float32),
            pltpu.VMEM((WIDE, WIDE), jnp.float32),
        ],
        compiler_params=pltpu.CompilerParams(vmem_limit_bytes=56 * 2**20),
        name="attend_back",
    )(ids, limits, glob, queries, kv, kv, grads, mixed, logs, head_mask)


def attention_tables(part, blocks, nblocks, group_flag, seq_lengths, random_ids):
    short_blocks = SHORT // BLOCK
    own = part * blocks + jnp.arange(blocks, dtype=jnp.int32)
    is_long = group_flag > 0
    member = jnp.where(is_long, 0, own // short_blocks)
    first = jnp.where(is_long, 0, member * short_blocks)
    span = jnp.where(is_long, nblocks, short_blocks)
    slots = jnp.arange(seq_lengths.shape[0], dtype=jnp.int32)
    valid = jnp.sum(jnp.where(member[:, None] == slots[None, :], seq_lengths[None, :], 0), axis=1)
    last = first + span - 1
    own_random = lax.dynamic_slice_in_dim(random_ids, part * blocks, blocks, 0)
    listed = jnp.concatenate(
        [jnp.stack([own - 1, own, own + 1], axis=1), own_random, jnp.stack([first, last], axis=1)],
        axis=1,
    )
    inside = (listed >= first[:, None]) & (listed <= last[:, None])
    column = jnp.arange(LISTED, dtype=jnp.int32)
    repeated = (column[None, :] >= 6) & (jnp.abs(listed - own[:, None]) <= 1)
    limits = valid[:, None] - (listed - first[:, None]) * BLOCK
    limits = jnp.where(inside & jnp.logical_not(repeated), limits, 0)
    ids = jnp.clip(listed, 0, nblocks - 1)
    is_edge = ((own == first) | (own == last)).astype(jnp.int32)
    chunks = jnp.broadcast_to(span * BLOCK // SPAN, own.shape)
    glob = jnp.stack([is_edge, first * BLOCK, chunks, valid], axis=1).astype(jnp.int32)
    return ids.reshape(-1), limits.astype(jnp.int32).reshape(-1), glob.reshape(-1)


def head_stack_mask():
    r = lax.broadcasted_iota(jnp.int32, (WIDE, WIDE), 0) // HEAD
    c = lax.broadcasted_iota(jnp.int32, (WIDE, WIDE), 1) // HEAD
    return (r == c).astype(jnp.bfloat16)


def plain_dot(left, right):
    return dot(left, right)


def left_dot(left, right):
    return dot(left, right, TN)


def right_dot(left, right):
    return dot(left, right, NT)


def normalize(values, norm_gain, norm_shift):
    centred = values - jnp.mean(values, axis=-1, keepdims=True)
    spread_inv = lax.rsqrt(jnp.mean(centred * centred, axis=-1, keepdims=True) + NORM_EPS)
    unit_value = centred * spread_inv
    return (unit_value * norm_gain + norm_shift, unit_value, spread_inv)


def normalize_back(grad_values, unit_value, spread_inv, norm_gain):
    scaled = grad_values * norm_gain
    centred = (
        scaled
        - jnp.mean(scaled, axis=-1, keepdims=True)
        - unit_value * jnp.mean(scaled * unit_value, axis=-1, keepdims=True)
    )
    return (
        spread_inv * centred,
        jnp.sum(grad_values * unit_value, axis=0),
        jnp.sum(grad_values, axis=0),
    )


def per_device(
    tokens,
    group_bucket,
    lengths,
    random_blocks,
    w_qkv,
    w_out,
    b_out,
    norm1_gain,
    norm1_shift,
    w_in,
    b_in,
    w_back,
    b_back,
    norm2_gain,
    norm2_shift,
    cotangent,
):
    low = jnp.bfloat16
    seq_parts = lax.axis_size("seq")
    part = lax.axis_index("seq")
    tok_rows, feat = tokens.shape
    blocks = tok_rows // BLOCK
    nblocks = blocks * seq_parts
    tables = attention_tables(
        part, blocks, nblocks, group_bucket[0], lengths[0], random_blocks[0]
    )
    head_mask = head_stack_mask()
    w_q, w_kv = w_qkv[:, :feat], w_qkv[:, feat:]
    inputs = tokens.astype(jnp.float32)
    group_tokens = lax.all_gather(tokens, "seq", axis=0, tiled=True)
    queries = plain_dot(tokens, w_q).astype(low) * low(HEAD ** (-0.5))
    kv = plain_dot(group_tokens, w_kv).astype(low)
    mixed, logs = attend(*tables, queries, kv, head_mask)

    branch = plain_dot(mixed, w_out) + b_out
    hidden, unit_first, spread_first = normalize(inputs + branch, norm1_gain, norm1_shift)
    hidden_low = hidden.astype(low)
    inner_pre = plain_dot(hidden_low, w_in) + b_in
    active, gelu_pull = jax.vjp(lambda value: jax.nn.gelu(value, approximate=False), inner_pre)
    active_low = active.astype(low)
    second = plain_dot(active_low, w_back) + b_back
    layer_out, unit_second, spread_second = normalize(hidden + second, norm2_gain, norm2_shift)
    grad_pre2, grad_gain2, grad_shift2 = normalize_back(
        cotangent.astype(jnp.float32), unit_second, spread_second, norm2_gain
    )
    grad_second = grad_pre2.astype(low)
    grad_w_back = left_dot(active_low, grad_second)
    grad_b_back = jnp.sum(grad_second.astype(jnp.float32), axis=0)
    grad_inner = gelu_pull(right_dot(grad_second, w_back))[0].astype(low)
    grad_w_in = left_dot(hidden_low, grad_inner)
    grad_b_in = jnp.sum(grad_inner.astype(jnp.float32), axis=0)
    grad_hidden = grad_pre2 + right_dot(grad_inner, w_in)
    grad_pre1, grad_gain1, grad_shift1 = normalize_back(
        grad_hidden, unit_first, spread_first, norm1_gain
    )
    grad_branch = grad_pre1.astype(low)
    grad_w_out = left_dot(mixed, grad_branch)
    grad_b_out = jnp.sum(grad_branch.astype(jnp.float32), axis=0)
    grad_mixed = right_dot(grad_branch, w_out).astype(low)

    both = ("batch", "seq")
    early = lax.psum((grad_w_in.astype(low), grad_w_back.astype(low), grad_w_out.astype(low)), both)
    dq, dk, dv = attend_back(*tables, queries, kv, grad_mixed, mixed, logs, head_mask)
    w_k, w_v = w_kv[:, :feat], w_kv[:, feat:]
    partial = (right_dot(dk, w_k) + right_dot(dv, w_v)).astype(low)
    summed_part = lax.psum_scatter(partial, "seq", scatter_dimension=0, tiled=True)
    grad_tokens = (
        grad_pre1 + right_dot(dq, w_q) + summed_part.astype(jnp.float32)
    ).astype(low)
    grad_w_qkv = jnp.concatenate(
        [left_dot(tokens, dq), left_dot(group_tokens, dk), left_dot(group_tokens, dv)], axis=1
    ).astype(low)
    late = lax.psum(grad_w_qkv, both)
    small = lax.psum(
        (
            grad_b_out,
            grad_gain1,
            grad_shift1,
            grad_b_in,
            grad_b_back,
            grad_gain2,
            grad_shift2,
        ),
        both,
    )
    wide = jnp.float32
    return (
        layer_out.astype(low),
        grad_tokens,
        late.astype(wide),
        early[2].astype(wide),
        small[0],
        small[1],
        small[2],
        early[0].astype(wide),
        small[3],
        early[1].astype(wide),
        small[4],
        small[5],
        small[6],
    )


def solution(mesh):
    rows = P(("batch", "seq"), None)
    whole = P()
    placed = (rows, P("batch"), P("batch", None), P("batch", None, None)) + (whole,) * 11 + (rows,)
    return jax.shard_map(
        per_device,
        mesh=mesh,
        in_specs=placed,
        out_specs=(rows, rows) + (whole,) * 11,
        check_vma=False,
    )
```

time: 2060 us -> 561 us (0.27)
  local copies, waits for them, and re-layouts: 927 us -> 16.4 us
  other arithmetic: 261 us -> 22.4 us
  waiting for transfers between devices: 470 us -> 250 us
  matrix products: 300 us -> 124 us
  Pallas kernels: 0 us -> 77.6 us
  starting transfers between devices: 21.8 us -> 0.12 us
    reshape x96 -> x1, local copies, waits for them, and re-layouts: 404 us -> 0.6 us  [attention_tables(): glob.reshape(-1)]
    gather x54 -> x0, local copies, waits for them, and re-layouts: 226 us -> none  [the longest x24 107 us: gather_blocks(): key_rows[:, span_listed]]
    psum x1, waiting for transfers between devices: 380 us -> 190 us  [per_device(): late = lax.psum(grad_w_qkv, both)]
    scatter-add x14 -> x0, other arithmetic: 188 us -> none  [the longest x6 91.1 us: one_span(): key_grad.at[:, span_listed]]
    dot_general x60 -> x17, matrix products: 300 us -> 124 us  [dot(): return lax.dot_general(a, b, dims, preferred_element_type=jnp.float32)]
    all_to_all x4 -> x0, waiting for transfers between devices: 90.2 us -> none  [the longest x1 49.6 us: per_device(): lax.all_to_all(stacked, 'seq', split_axis=0, concat_axis=2, tiled=True)]
    pallas_call x0 -> x2, Pallas kernels: none -> 77.6 us  [the longest x1 42 us: attend_back(): pl.pallas_call(functools.partial(attend_back_kernel, blocks), grid=(quads...]
    while x78 -> x0, local copies, waits for them, and re-layouts: 39.3 us -> none
  transfers between devices with their start and end apart: 5 -> 3, of which waited for: 5 -> 3; matrix products, arithmetic and copies ran while one was open for 3% -> 9% of each run, Pallas kernels for 0% -> 0%
where the time goes in v1:
time: 561 us; the launch traced here: 552 us
  waiting for transfers between devices  250 us (45%)
  matrix products  124 us (22%)
  Pallas kernels  77.6 us (14%)
  blocking collectives  46.9 us (8%)
  other arithmetic  22.4 us (4%)
  local copies, waits for them, and re-layouts  16.4 us (3%)
  between operations  15.3 us (3%)
    psum x1, waiting for transfers between devices, per_device(): late = lax.psum(grad_w_qkv, both)  190 us
    dot_general x17, matrix products, dot(): return lax.dot_general(a, b, dims, preferred_element_type=jnp.float32)  124 us
    psum x1, blocking collectives, per_device(): lax.psum((grad_b_out, grad_gain1, grad_shift1, grad_b_in, grad_b_back, gr...  46.9 us
    pallas_call x1, Pallas kernels, attend_back(): pl.pallas_call(functools.partial(attend_back_kernel, blocks), grid=(quads...  42 us
    pallas_call x1, Pallas kernels, attend(): pl.pallas_call(functools.partial(attend_kernel, blocks), grid=(quads,), o...  35.7 us
    reduce_scatter x1, waiting for transfers between devices, per_device(): lax.psum_scatter(partial, 'seq', scatter_dimension=0, tiled=True)  30.1 us
    all_gather x1, waiting for transfers between devices, per_device(): group_tokens = lax.all_gather(tokens, 'seq', axis=0, tiled=True)  28.9 us
    unnamed x64, local copies, waits for them, and re-layouts  14.2 us
  transfers between devices with their start and end apart: 3, of which 3 were waited for; matrix products, arithmetic and copies ran while one was open for 9% of the time, Pallas kernels for 0%

profile of v1, /device:TPU:25, one launch (start us, length us, event | category | flops | bytes accessed | tf_op | source)
XLA Modules:
  0.0 552.1 jit_solution(6353851054869120428)
XLA Ops:
  16.1 3.5 fusion.15.q_ref
  19.6 28.9 %all-gather.2.cloned.1.call-done = bf16[3072,768]{1,0:T(8,128)(2,1)} async-done(((bf16[768,768]{1,0:T(8,128)(2,1)}), bf16[3072,768]{1,0:T(8,128)(2,1)}) %all-gather.2.cloned.1.call-update) | async-done | bytes 4718608 | tf_op jit(solution)/shard_map/all_gather | solution.py:367
  48.5 12.6 %convolution_convert_fusion.k_ref.v_ref = bf16[3072,1536]{1,0:T(8,128)(2,1)} fusion(bf16[3072,768]{1,0:T(8,128)(2,1)} %all-gather.2.cloned.1.call-done, bf16[768,2304]{1,0:T(8,128)(2,1)} %param.20), kind=kOutput, calls=%fused_computation.1 | convolution fusion | flops 7252475904 | bytes 16515072 | tf_op jit(solution)/shard_map/dot_general | solution.py:24
  61.1 35.7 %attend.1 = (bf16[768,768]{1,0:T(8,128)(2,1)}, f32[3,16,256]{2,1,0:T(8,128)}) custom-call(s32[96]{0:T(128)} %min.12.ids_ref, s32[96]{0:T(128)} %reshape.213.lim_ref, s32[48]{0:T(128)} %reshape.209.glob_ref, bf16[768,768]{1,0:T(8,128)(2,1)} %fusion.15.q_ref, bf16[3072,1536]{1,0:T(8,128)(2,1)} %convolution_convert_fusion.k_ref.v_ref, ...), custom_call_target="tpu_custom_call" | custom-call | tf_op jit(solution)/shard_map/attend/pallas_call | solution.py:121
  96.8 2.7 fusion.37
  100.3 28.7 %multiply_convert_fusion = (bf16[768,3072]{1,0:T(8,128)(2,1)S(1)}, f32[768,3072]{1,0:T(8,128)}, f32[768,3072]{1,0:T(8,128)}) fusion(f32[3072]{0:T(1024)S(1)} %copy-done.13, bf16[768,3072]{1,0:T(8,128)(2,1)S(1)} %bitcast.45, f32[768,768]{0,1:T(8,128)S(1)} %get-tuple-element.99, f32[768]{0:T(1024)S(1)} %copy-done.16, f32[768]{0:T(1024)S(1)} %copy-done.9, ...), kind=kOutput, calls=%fused_computation.6 | convolution fusion | flops 3782541312 | bytes 30695424 | tf_op jit(solution)/shard_map/dot_general | solution.py:24
  129.0 4.8 fusion.38
  136.8 5.7 %convolution_convert_fusion.1 = bf16[3072,768]{1,0:T(8,128)(2,1)} fusion(bf16[768,3072]{1,0:T(8,128)(2,1)S(1)} %get-tuple-element.87, bf16[768,768]{0,1:T(8,128)(2,1)S(1)} %get-tuple-element.82), kind=kOutput, calls=%fused_computation.20 | convolution fusion | flops 3626237952 | bytes 10616832 | tf_op jit(solution)/shard_map/dot_general | solution.py:24
  142.5 13.0 %convert_reduce_fusion = (f32[3072]{0:T(1024)}, bf16[768,3072]{1,0:T(8,128)(2,1)}) fusion(f32[768,3072]{1,0:T(8,128)} %get-tuple-element.88, f32[768,3072]{1,0:T(8,128)} %get-tuple-element.100, f32[3072]{0:T(1024)S(1)} %copy-done.13, bf16[768,768]{0,1:T(8,128)(2,1)S(1)} %get-tuple-element.82, bf16[3072,768]{1,0:T(8,128)(2,1)S(1)} %bitcast.43), kind=kOutput, calls=%fused_computation.3 | convolution fusion | flops 3663983616 | bytes 29515776 | tf_op jit(solution)/shard_map/dot_general | solution.py:24
  155.5 9.6 %multiply_reduce_fusion = (f32[768]{0:T(1024)S(1)}, f32[768]{0:T(1024)S(1)}, f32[768]{0:T(1024)S(1)}, f32[768]{0:T(1024)}, f32[768,768]{0,1:T(8,128)S(1)}) fusion(f32[768,768]{0,1:T(8,128)S(1)} %get-tuple-element.99, f32[768]{0:T(1024)S(1)} %add_rsqrt_fusion.1, f32[768]{0:T(1024)S(1)} %broadcast_multiply_fusion.5, f32[768]{0:T(1024)S(1)} %copy-done.9, ...), kind=kOutput, calls=%fused_computation.34 | convolution fusion | flops 3634492416 | bytes 17731584 | tf_op jit(solution)/shard_map/dot_general | solution.py:24
  165.0 5.9 %convolution_convert_fusion.2 = bf16[768,3072]{1,0:T(8,128)(2,1)} fusion(bf16[768,3072]{1,0:T(8,128)(2,1)S(1)} %copy-done.18, f32[768,768]{0,1:T(8,128)S(1)} %get-tuple-element.99, f32[768]{0:T(1024)S(1)} %copy-done.16, f32[768]{0:T(1024)S(1)} %copy-done.9, f32[768]{0:T(1024)S(1)} %add_rsqrt_fusion.1, f32[768]{0:T(1024)S(1)} %broadcast_multiply_fusion.5), kind=kOutput, calls=%fused_computation.21 | convolution fusion | flops 3629187072 | bytes 11808768 | tf_op jit(solution)/shard_map/dot_general | solution.py:24
  176.5 42.0 %attend_back.1 = (bf16[768,768]{1,0:T(8,128)(2,1)}, bf16[3072,768]{1,0:T(8,128)(2,1)}, bf16[3072,768]{1,0:T(8,128)(2,1)}) custom-call(s32[96]{0:T(128)} %min.12.ids_ref, s32[96]{0:T(128)} %reshape.213.lim_ref, s32[48]{0:T(128)} %reshape.209.glob_ref, bf16[768,768]{1,0:T(8,128)(2,1)} %fusion.15.q_ref, bf16[3072,1536]{1,0:T(8,128)(2,1)} %convolution_convert_fusion.k_ref.v_ref, ...), custom_call_target="tpu_custom_call" | custom-call | tf_op jit(solution)/shard_map/attend_back/pallas_call | solution.py:238
  221.1 7.9 %fusion.17 = bf16[768,768]{0,1:T(8,128)(2,1)S(1)} fusion(bf16[3072,768]{1,0:T(8,128)(2,1)} %get-tuple-element.21, bf16[3072,768]{1,0:T(8,128)(2,1)} %all-gather.2.cloned.1.call-done), kind=kOutput, calls=%fused_computation.59 | convolution fusion | flops 3624468480 | bytes 10616832 | tf_op jit(solution)/shard_map/dot_general | solution.py:24
  229.1 4.0 fusion.18
  235.1 6.3 %fusion.20 = f32[3072,768]{0,1:T(8,128)S(1)} fusion(bf16[3072,768]{1,0:T(8,128)(2,1)} %get-tuple-element.21, bf16[768,2304]{1,0:T(8,128)(2,1)} %param.20), kind=kOutput, calls=%fused_computation.62 | convolution fusion | flops 3623878656 | bytes 15335424 | tf_op jit(solution)/shard_map/dot_general | solution.py:24
  241.4 8.8 %add_convert_fusion = bf16[3072,768]{0,1:T(8,128)(2,1)} fusion(f32[3072,768]{0,1:T(8,128)S(1)} %fusion.20, bf16[3072,768]{1,0:T(8,128)(2,1)} %get-tuple-element.22, bf16[768,2304]{1,0:T(8,128)(2,1)} %param.20), kind=kOutput, calls=%fused_computation.4 | convolution fusion | flops 3628597248 | bytes 20054016 | tf_op jit(solution)/shard_map/dot_general | solution.py:24
  251.7 46.9 %all-reduce = (f32[768]{0:T(1024)}, f32[768]{0:T(1024)}, f32[768]{0:T(1024)}, f32[3072]{0:T(1024)}, f32[768]{0:T(1024)}, /*index=5*/f32[768]{0:T(1024)}, f32[768]{0:T(1024)}) all-reduce(f32[768]{0:T(1024)S(1)} %get-tuple-element.85, f32[768]{0:T(1024)S(1)} %get-tuple-element.62, ...), channel_id=1, replica_groups=mesh['batch'=8,'seq'=4] {'batch','seq'}, use_global_device_ids=true, to_apply=%region_13.14 | all-reduce | flops 7680 | bytes 61440 | tf_op jit(solution)/shard_map/psum | solution.py:411
  298.6 189.9 %all-reduce.4.cloned.1.call-done = (bf16[768,2304]{0,1:T(8,128)(2,1)}, bf16[768,768]{1,0:T(8,128)(2,1)}, bf16[768,3072]{1,0:T(8,128)(2,1)}, bf16[3072,768]{1,0:T(8,128)(2,1)}) async-done(((bf16[768,2304]{0,1:T(8,128)(2,1)}, bf16[768,768]{1,0:T(8,128)(2,1)}, bf16[768,3072]{1,0:T(8,128)(2,1)}, bf16[3072,768]{1,0:T(8,128)(2,1)}), (bf16[768,2304]{0,1:T(8,128)(2,1)}, bf16[768,768]{1,0:T(8,128)(2,1)}, ...) | async-done | bytes 14155792 | tf_op jit(solution)/shard_map/psum | solution.py:410
  488.5 2.8 convert_element_type.106
  491.4 6.0 %copy.67 = f32[768,2304]{1,0:T(8,128)} copy(bf16[768,2304]{0,1:T(8,128)(2,1)} %get-tuple-element.77) | data formatting | bytes 10616832
  497.4 8.3 %convert_element_type.109 = f32[768,3072]{1,0:T(8,128)} convert(bf16[768,3072]{1,0:T(8,128)(2,1)} %get-tuple-element.79) | non-fusion elementwise | flops 2359296 | bytes 14155776 | tf_op jit(solution)/shard_map/convert_element_type | solution.py:432
  505.7 4.5 convert_element_type.112
  510.2 30.1 %reduce-scatter.2.cloned.1.call-done = bf16[768,768]{0,1:T(8,128)(2,1)} async-done(((bf16[3072,768]{0,1:T(8,128)(2,1)}), bf16[768,768]{0,1:T(8,128)(2,1)}) %reduce-scatter.2.cloned.1.call-update) | async-done | bytes 1179664 | tf_op jit(solution)/shard_map/reduce_scatter | solution.py:403
  540.2 3.5 add_convert_fusion.2
  (112 shorter events, 24.9 us)
Async XLA Ops:
  7.2 89.6 %copy-start = (bf16[768,768]{1,0:T(8,128)(2,1)S(1)}, bf16[768,768]{1,0:T(8,128)(2,1)}, u32[]{:S(2)}) copy-start(bf16[768,768]{1,0:T(8,128)(2,1)} %param.21) | copy-start | bytes 3538948
  7.2 4.0 copy-start.11
  7.2 4.2 copy-start.17
  7.2 41.3 %all-gather.2.cloned.1.call-start = ((), (), s32[]{:S(2)}) async-start(), calls=%async_computation.1 | async-start | bytes 5898240 | tf_op jit(solution)/shard_map/all_gather | solution.py:367
  7.9 480.6 %all-reduce.4.cloned.1.call-start = ((), (), s32[]{:S(2)}) async-start(), calls=%async_computation.3 | async-start | bytes 28311552 | tf_op jit(solution)/shard_map/psum | solution.py:410
  8.7 7.5 %copy-start.1 = (bf16[768,768]{1,0:T(8,128)(2,1)S(1)}, bf16[768,768]{1,0:T(8,128)(2,1)}, u32[]{:S(2)}) copy-start(bf16[768,768]{1,0:T(8,128)(2,1)} %param.16) | copy-start | bytes 3538948
  61.1 35.7 %copy-start.5 = (bf16[768,768]{0,1:T(8,128)(2,1)S(1)}, bf16[768,768]{0,1:T(8,128)(2,1)}, u32[]{:S(2)}) copy-start(bf16[768,768]{0,1:T(8,128)(2,1)} %copy.55) | copy-start | bytes 3538948
  61.1 35.7 %copy-start.14 = (f32[768]{0:T(1024)S(1)}, f32[768]{0:T(1024)}, u32[]{:S(2)}) copy-start(f32[768]{0:T(1024)} %param.22) | copy-start | bytes 9220
  96.8 3.1 slice-start.4
  96.8 3.1 slice-start.5
  96.8 32.2 %slice-start.2 = ((s8[4718592]{0:T(1024)(128)(4,1)}), s8[524288]{0:T(1024)(128)(4,1)S(1)}, s32[]{:S(2)}) async-start(s8[4718592]{0:T(1024)(128)(4,1)} %bitcast.42), calls=%async_computation.6 | async-start | bytes 1048576
  100.3 28.8 %slice-start.3 = ((s8[4718592]{0:T(1024)(128)(4,1)}), s8[4194304]{0:T(1024)(128)(4,1)S(1)}, s32[]{:S(2)}) async-start(s8[4718592]{0:T(1024)(128)(4,1)} %bitcast.42), calls=%async_computation.7 | async-start | bytes 8388608
  100.3 28.8 %copy-start.15 = (f32[768]{0:T(1024)S(1)}, f32[768]{0:T(1024)}, u32[]{:S(2)}) copy-start(f32[768]{0:T(1024)} %param.28) | copy-start | bytes 9220
  155.4 9.6 %copy-start.18 = (bf16[768,3072]{1,0:T(8,128)(2,1)S(1)}, bf16[768,3072]{1,0:T(8,128)(2,1)}, u32[]{:S(2)}) copy-start(bf16[768,3072]{1,0:T(8,128)(2,1)} %get-tuple-element.84) | copy-start | bytes 14155780
  171.8 2.5 copy-start.3
  176.5 42.0 %copy-start.2 = (bf16[768,768]{1,0:T(8,128)(2,1)S(1)}, bf16[768,768]{1,0:T(8,128)(2,1)}, u32[]{:S(2)}) copy-start(bf16[768,768]{1,0:T(8,128)(2,1)} %param.16) | copy-start | bytes 3538948
  218.5 10.5 %slice-start.6 = ((s8[4718592]{0:T(1024)(128)(4,1)}), s8[4194304]{0:T(1024)(128)(4,1)S(1)}, s32[]{:S(2)}) async-start(s8[4718592]{0:T(1024)(128)(4,1)} %bitcast.46), calls=%async_computation.10 | async-start | bytes 8388608
  218.5 10.5 %slice-start.8 = ((s8[4718592]{0:T(1024)(128)(4,1)}), s8[4194304]{0:T(1024)(128)(4,1)S(1)}, s32[]{:S(2)}) async-start(s8[4718592]{0:T(1024)(128)(4,1)} %bitcast.48), calls=%async_computation.12 | async-start | bytes 8388608
  221.1 8.0 %slice-start.7 = ((s8[4718592]{0:T(1024)(128)(4,1)}), s8[524288]{0:T(1024)(128)(4,1)S(1)}, s32[]{:S(2)}) async-start(s8[4718592]{0:T(1024)(128)(4,1)} %bitcast.46), calls=%async_computation.11 | async-start | bytes 1048576
  221.1 8.0 %slice-start.9 = ((s8[4718592]{0:T(1024)(128)(4,1)}), s8[524288]{0:T(1024)(128)(4,1)S(1)}, s32[]{:S(2)}) async-start(s8[4718592]{0:T(1024)(128)(4,1)} %bitcast.48), calls=%async_computation.13 | async-start | bytes 1048576
  235.1 305.2 %reduce-scatter.2.cloned.1.call-start = ((), (), s32[]{:S(2)}) async-start(), calls=%async_computation.2 | async-start | bytes 5898240 | tf_op jit(solution)/shard_map/reduce_scatter | solution.py:403
  491.4 14.3 %slice-start = ((s8[4718592]{0:T(1024)(128)(4,1)}), s8[524288]{0:T(1024)(128)(4,1)S(1)}, s32[]{:S(2)}) async-start(s8[4718592]{0:T(1024)(128)(4,1)} %bitcast.38), calls=%async_computation.4 | async-start | bytes 1048576
  497.4 8.3 %slice-start.1 = ((s8[4718592]{0:T(1024)(128)(4,1)}), s8[4194304]{0:T(1024)(128)(4,1)S(1)}, s32[]{:S(2)}) async-start(s8[4718592]{0:T(1024)(128)(4,1)} %bitcast.38), calls=%async_computation.5 | async-start | bytes 8388608
  505.7 34.5 %copy-start.12 = (bf16[768,768]{1,0:T(8,128)(2,1)S(1)}, bf16[768,768]{1,0:T(8,128)(2,1)}, u32[]{:S(2)}) copy-start(bf16[768,768]{1,0:T(8,128)(2,1)} %get-tuple-element.20) | copy-start | bytes 3538948
  (8 other events, 8.5 us)
Sparse Core Ops, SparseCore 0:
  9.6 38.8 all-gather.1
  235.2 253.3 all-reduce.3
  491.1 49.0 reduce-scatter.1

commit v2 on v1

--- a/solution.py
+++ b/solution.py
@@ -300,6 +300,303 @@
     c = lax.broadcasted_iota(jnp.int32, (WIDE, WIDE), 1) // HEAD
     return (r == c).astype(jnp.bfloat16)
 
+BLOCK8 = 8
+
+
+def finish_kernel(
+    cut, w_in_ref, w_back_ref, w_out_ref, small_ref, dq_ref, dk_ref, dv_ref, tok_ref, w_ref, pre_ref,
+    out_ref, gtok_ref, sum_ref,
+    work, got0, got1, got2, got3, piece, slabs, part, part_in, total_ref, small_in,
+    send_sem, recv_sem, local_sem,
+):
+    batch, seq = lax.axis_index("batch"), lax.axis_index("seq")
+    inner = lax.rem(batch, BLOCK8)
+    base = batch - inner
+    x, z = lax.rem(inner, 2), lax.div(inner, 2)
+    core, y = lax.rem(seq, 2), lax.div(seq, 2)
+
+    def device(z, x, y, core):
+        return (base + z * 2 + x, y * 2 + core)
+
+    sibling = device(z, x, y, 1 - core)
+    over_x = device(z, 1 - x, y, core)
+    over_y = device(z, x, 1 - y, core)
+    over_z = [device(lax.rem(z + k, 4), x, y, core) for k in (1, 2, 3)]
+    partners = [sibling, over_x, over_y] + over_z
+    barrier = pltpu.get_barrier_semaphore()
+    for other in partners:
+        pl.semaphore_signal(barrier, inc=1, device_id=other, device_id_type=pl.DeviceIdType.MESH)
+    pl.semaphore_wait(barrier, len(partners))
+
+    tick = [0, 0]
+
+    def send(src, dst, other, keep=True):
+        k = tick[0]
+        tick[0] += 1
+        copy = pltpu.make_async_remote_copy(
+            src_ref=src,
+            dst_ref=dst,
+            send_sem=send_sem.at[k],
+            recv_sem=recv_sem.at[k],
+            device_id=other,
+            device_id_type=pl.DeviceIdType.MESH,
+        )
+        copy.start()
+        if keep:
+            started.append(copy)
+        return copy
+
+    def local(src, dst):
+        k = tick[1]
+        tick[1] += 1
+        copy = pltpu.make_async_copy(src, dst, local_sem.at[k])
+        copy.start()
+        return copy
+
+    started = []
+    rows, feat = gtok_ref.shape
+    half = rows // 2
+    quarter = half // 4
+    mine = pl.multiple_of(core * half, half)
+    theirs = pl.multiple_of((1 - core) * half, half)
+    own = x * 2 + y
+    columns = [pl.ds(0, cut), pl.ds(cut, feat - cut)]
+
+    def add_rows(dst, src, count, step=64):
+        def one(i, carry):
+            at = pl.ds(pl.multiple_of(i * step, step), step)
+            dst[at, :] = dst[at, :] + src[at, :]
+            return carry
+
+        lax.fori_loop(0, count // step, one, 0)
+
+    def first_step(k, n, src):
+        away = send(src.at[pl.ds(theirs, half), :], got0.at[k, n], sibling)
+        here = local(src.at[pl.ds(mine, half), :], work.at[k, n])
+        return away, here
+
+    def first_sum(k, n, pair):
+        away, here = pair
+        here.wait()
+        away.wait_recv()
+        add_rows(work.at[k, n], got0.at[k, n], half)
+
+    def second_step(k):
+        a = [
+            send(work.at[k, 2 * (1 - x) + j, :, columns[0]], got1.at[k, j, :, columns[0]], over_x)
+            for j in range(2)
+        ]
+        b = [
+            send(work.at[k, 2 * j + 1 - y, :, columns[1]], got1.at[k, j, :, columns[1]], over_y)
+            for j in range(2)
+        ]
+        return a, b
+
+    def third_step(k, moves):
+        a, b = moves
+        for j in range(2):
+            a[j].wait_recv()
+            add_rows(work.at[k, 2 * x + j, :, columns[0]], got1.at[k, j, :, columns[0]], half)
+        nxt_a = send(
+            work.at[k, 2 * x + 1 - y, :, columns[0]], got2.at[k, :, columns[0]], over_y
+        )
+        for j in range(2):
+            b[j].wait_recv()
+            add_rows(work.at[k, 2 * j + y, :, columns[1]], got1.at[k, j, :, columns[1]], half)
+        nxt_b = send(
+            work.at[k, 2 * (1 - x) + y, :, columns[1]], got2.at[k, :, columns[1]], over_x
+        )
+        return nxt_a, nxt_b
+
+    def fourth_step(k, moves):
+        for move, column in zip(moves, columns):
+            move.wait_recv()
+            add_rows(work.at[k, own, :, column], got2.at[k, :, column], half)
+        return [
+            send(
+                work.at[k, own, pl.ds(pl.multiple_of(lax.rem(z + d, 4) * quarter, quarter), quarter), :],
+                got3.at[k, d - 1],
+                over_z[d - 1],
+            )
+            for d in (1, 2, 3)
+        ]
+
+    def spread_z(k, moves):
+        for move in moves:
+            move.wait_recv()
+        total = work[k, own, pl.ds(pl.multiple_of(z * quarter, quarter), quarter), :].astype(jnp.float32)
+        for d in range(3):
+            total = total + got3[k, d].astype(jnp.float32)
+        piece[k] = total.astype(jnp.bfloat16)
+        place = out_ref.at[k, own, pl.ds(pl.multiple_of(mine + z * quarter, quarter), quarter), :]
+        return [send(piece.at[k], place, other) for other in over_z] + [local(piece.at[k], place)]
+
+    def spread_second(k, moves):
+        for move in moves[:3]:
+            move.wait_recv()
+        moves[3].wait()
+        a = out_ref.at[k, own, pl.ds(mine, half), columns[0]]
+        b = out_ref.at[k, own, pl.ds(mine, half), columns[1]]
+        return send(a, a, over_y), send(b, b, over_x)
+
+    def spread_third(k, moves):
+        moves[0].wait_recv()
+        moves[1].wait_recv()
+        result = []
+        for j in range(2):
+            a = out_ref.at[k, 2 * x + j, pl.ds(mine, half), columns[0]]
+            result.append(send(a, a, over_x))
+        for j in range(2):
+            b = out_ref.at[k, 2 * j + y, pl.ds(mine, half), columns[1]]
+            result.append(send(b, b, over_y))
+        return result
+
+    def spread_cores(k, moves):
+        for move in moves:
+            move.wait_recv()
+        place = out_ref.at[k, :, pl.ds(mine, half), :]
+        return send(place, place, sibling)
+
+    def small_step(s, other):
+        move = send(sum_ref if s else small_ref, small_in.at[s], other, False)
+        return move
+
+    def small_add(s, move):
+        move.wait()
+        sum_ref[...] = (sum_ref if s else small_ref)[...] + small_in[s]
+
+    small_partners = [
+        sibling,
+        over_x,
+        over_y,
+        device(z + 1 - 2 * lax.rem(z, 2), x, y, core),
+        device(lax.rem(z + 2, 4), x, y, core),
+    ]
+
+    def token_part(py, pc):
+        at = pl.ds(pl.multiple_of((py * 2 + pc) * rows, rows), rows)
+        return dot(dk_ref[at, :], w_ref[:, feat : 2 * feat], NT) + dot(
+            dv_ref[at, :], w_ref[:, 2 * feat : 3 * feat], NT
+        )
+
+    def weight_rows(columns_at, store):
+        at = pl.ds(pl.multiple_of(seq * rows, rows), rows)
+        store(0, dot(tok_ref[at, columns_at], dq_ref[...], TN).astype(jnp.bfloat16))
+        store(1, dot(tok_ref[:, columns_at], dk_ref[...], TN).astype(jnp.bfloat16))
+        store(2, dot(tok_ref[:, columns_at], dv_ref[...], TN).astype(jnp.bfloat16))
+
+    pre_copy = local(pre_ref, total_ref)
+    firsts = [[first_step(k, n, src.at[n]) for n in range(4)] for k, src in ((0, w_in_ref), (1, w_back_ref))]
+    out_first = first_step(2, 3, w_out_ref)
+    small_move = small_step(0, small_partners[0])
+    part[0] = token_part(1 - y, 1 - core).astype(jnp.bfloat16)
+    far = send(part.at[0], part_in.at[0], sibling)
+    for n in range(4):
+        first_sum(0, n, firsts[0][n])
+    seconds = [second_step(0), None, None]
+    part[1] = token_part(y, 1 - core).astype(jnp.bfloat16)
+    near = send(part.at[1], part_in.at[1], sibling)
+    for n in range(4):
+        first_sum(1, n, firsts[1][n])
+    seconds[1] = second_step(1)
+    small_add(0, small_move)
+    small_move = small_step(1, small_partners[1])
+    part[2] = token_part(1 - y, core).astype(jnp.bfloat16)
+    far.wait_recv()
+    add_rows(part.at[2], part_in.at[0], rows)
+    cross = send(part.at[2], part_in.at[2], over_y)
+
+    def store_away(n, value):
+        slabs[n] = value
+
+    def store_here(n, value):
+        work[2, n] = value
+
+    weight_rows(pl.ds(theirs, half), store_away)
+    away = [send(slabs.at[n], got0.at[2, n], sibling) for n in range(3)]
+    thirds = [third_step(0, seconds[0]), None, None]
+    weight_rows(pl.ds(mine, half), store_here)
+    thirds[1] = third_step(1, seconds[1])
+    small_add(1, small_move)
+    small_move = small_step(2, small_partners[2])
+    for n in range(3):
+        away[n].wait_recv()
+        add_rows(work.at[2, n], got0.at[2, n], half)
+    first_sum(2, 3, out_first)
+    seconds[2] = second_step(2)
+    fourths = [fourth_step(0, thirds[0]), None, None]
+    pre_copy.wait()
+    total_ref[...] = (
+        total_ref[...] + dot(dq_ref[...], w_ref[:, 0:feat], NT) + token_part(y, core)
+    )
+    fourths[1] = fourth_step(1, thirds[1])
+    spreads = [spread_z(0, fourths[0]), None, None]
+    small_add(2, small_move)
+    small_move = small_step(3, small_partners[3])
+    thirds[2] = third_step(2, seconds[2])
+    spreads[1] = spread_z(1, fourths[1])
+    seconds_out = [spread_second(0, spreads[0]), None, None]
+    small_add(3, small_move)
+    small_move = small_step(4, small_partners[4])
+    fourths[2] = fourth_step(2, thirds[2])
+    seconds_out[1] = spread_second(1, spreads[1])
+    thirds_out = [spread_third(0, seconds_out[0]), None, None]
+    spreads[2] = spread_z(2, fourths[2])
+    thirds_out[1] = spread_third(1, seconds_out[1])
+    lasts = [spread_cores(0, thirds_out[0])]
+    seconds_out[2] = spread_second(2, spreads[2])
+    small_add(4, small_move)
+    thirds_out[2] = spread_third(2, seconds_out[2])
+    lasts.append(spread_cores(1, thirds_out[1]))
+    near.wait_recv()
+    cross.wait_recv()
+    gtok_ref[...] = (
+        total_ref[...] + part_in[1].astype(jnp.float32) + part_in[2].astype(jnp.float32)
+    ).astype(jnp.bfloat16)
+    lasts.append(spread_cores(2, thirds_out[2]))
+    for move in lasts:
+        move.wait_recv()
+    for copy in started:
+        copy.wait_send()
+
+
+def finish(w_in_grad, w_back_grad, w_out_grad, small, dq, dk, dv, group_tokens, w_qkv, grad_pre1):
+    rows, feat = dq.shape
+    half = rows // 2
+    low = jnp.bfloat16
+    vmem = pl.BlockSpec(memory_space=pltpu.VMEM)
+    anywhere = pl.BlockSpec(memory_space=pl.ANY)
+    return pl.pallas_call(
+        functools.partial(finish_kernel, feat // 2),
+        out_shape=(
+            jax.ShapeDtypeStruct((3, 4, rows, feat), low),
+            jax.ShapeDtypeStruct((rows, feat), low),
+            jax.ShapeDtypeStruct(small.shape, jnp.float32),
+        ),
+        in_specs=[anywhere, anywhere, anywhere, vmem, vmem, vmem, vmem, vmem, vmem, anywhere],
+        out_specs=(anywhere, vmem, vmem),
+        scratch_shapes=[
+            pltpu.VMEM((3, 4, half, feat), low),
+            pltpu.VMEM((3, 4, half, feat), low),
+            pltpu.VMEM((3, 2, half, feat), low),
+            pltpu.VMEM((3, half, feat), low),
+            pltpu.VMEM((3, 3, half // 4, feat), low),
+            pltpu.VMEM((3, half // 4, feat), low),
+            pltpu.VMEM((3, half, feat), low),
+            pltpu.VMEM((3, rows, feat), low),
+            pltpu.VMEM((3, rows, feat), low),
+            pltpu.VMEM((rows, feat), jnp.float32),
+            pltpu.VMEM((5,) + small.shape, jnp.float32),
+            pltpu.SemaphoreType.DMA((128,)),
+            pltpu.SemaphoreType.DMA((128,)),
+            pltpu.SemaphoreType.DMA((32,)),
+        ],
+        compiler_params=pltpu.CompilerParams(
+            collective_id=0, has_side_effects=True, vmem_limit_bytes=60 * 2**20
+        ),
+        name="finish",
+    )(w_in_grad, w_back_grad, w_out_grad, small, dq, dk, dv, group_tokens, w_qkv, grad_pre1)
+
 
 def plain_dot(left, right):
     return dot(left, right)
@@ -381,60 +678,65 @@
         cotangent.astype(jnp.float32), unit_second, spread_second, norm2_gain
     )
     grad_second = grad_pre2.astype(low)
-    grad_w_back = left_dot(active_low, grad_second)
+    grad_w_back = left_dot(active_low, grad_second).astype(low).reshape(4, tok_rows, feat)
     grad_b_back = jnp.sum(grad_second.astype(jnp.float32), axis=0)
     grad_inner = gelu_pull(right_dot(grad_second, w_back))[0].astype(low)
-    grad_w_in = left_dot(hidden_low, grad_inner)
+    grad_w_in = jnp.stack(
+        [left_dot(hidden_low, grad_inner[:, n * feat : (n + 1) * feat]).astype(low) for n in range(4)]
+    )
     grad_b_in = jnp.sum(grad_inner.astype(jnp.float32), axis=0)
     grad_hidden = grad_pre2 + right_dot(grad_inner, w_in)
     grad_pre1, grad_gain1, grad_shift1 = normalize_back(
         grad_hidden, unit_first, spread_first, norm1_gain
     )
     grad_branch = grad_pre1.astype(low)
-    grad_w_out = left_dot(mixed, grad_branch)
+    grad_w_out = left_dot(mixed, grad_branch).astype(low)
     grad_b_out = jnp.sum(grad_branch.astype(jnp.float32), axis=0)
     grad_mixed = right_dot(grad_branch, w_out).astype(low)
 
-    both = ("batch", "seq")
-    early = lax.psum((grad_w_in.astype(low), grad_w_back.astype(low), grad_w_out.astype(low)), both)
+    def fold(value):
+        return jnp.pad(value.reshape(-1, feat), ((0, 0), (0, 0)))
+
+    small = jnp.concatenate(
+        [
+            fold(v)
+            for v in (
+                grad_b_out, grad_gain1, grad_shift1, grad_b_back, grad_gain2, grad_shift2, grad_b_in,
+            )
+        ],
+        axis=0,
+    )
+    used = small.shape[0]
+    small = jnp.pad(small, ((0, 16 - used), (0, 0)))
     dq, dk, dv = attend_back(*tables, queries, kv, grad_mixed, mixed, logs, head_mask)
-    w_k, w_v = w_kv[:, :feat], w_kv[:, feat:]
-    partial = (right_dot(dk, w_k) + right_dot(dv, w_v)).astype(low)
-    summed_part = lax.psum_scatter(partial, "seq", scatter_dimension=0, tiled=True)
-    grad_tokens = (
-        grad_pre1 + right_dot(dq, w_q) + summed_part.astype(jnp.float32)
-    ).astype(low)
-    grad_w_qkv = jnp.concatenate(
-        [left_dot(tokens, dq), left_dot(group_tokens, dk), left_dot(group_tokens, dv)], axis=1
-    ).astype(low)
-    late = lax.psum(grad_w_qkv, both)
-    small = lax.psum(
-        (
-            grad_b_out,
-            grad_gain1,
-            grad_shift1,
-            grad_b_in,
-            grad_b_back,
-            grad_gain2,
-            grad_shift2,
-        ),
-        both,
+    grads, grad_tokens, sums = finish(
+        grad_w_in, grad_w_back, grad_w_out, small, dq, dk, dv, group_tokens, w_qkv, grad_pre1
     )
     wide = jnp.float32
+    outer = lax.axis_size("batch") // BLOCK8
+    if outer > 1:
+        groups = [[o * BLOCK8 + i for o in range(outer)] for i in range(BLOCK8)]
+        grads = lax.psum(grads.astype(wide), "batch", axis_index_groups=groups)
+        sums = lax.psum(sums, "batch", axis_index_groups=groups)
+    grads = grads.astype(wide)
+    full_in = grads[0].transpose(1, 0, 2).reshape(w_in.shape)
+    full_back = grads[1].reshape(w_back.shape)
+    full_qkv = grads[2, :3].transpose(1, 0, 2).reshape(w_qkv.shape)
+    full_out = grads[2, 3]
     return (
         layer_out.astype(low),
         grad_tokens,
-        late.astype(wide),
-        early[2].astype(wide),
-        small[0],
-        small[1],
-        small[2],
-        early[0].astype(wide),
-        small[3],
-        early[1].astype(wide),
-        small[4],
-        small[5],
-        small[6],
+        full_qkv,
+        full_out,
+        sums[0],
+        sums[1],
+        sums[2],
+        full_in,
+        sums[6:10].reshape(b_in.shape),
+        full_back,
+        sums[3],
+        sums[4],
+        sums[5],
     )
 
 

time: 561 us -> 516 us (0.920)
  waiting for transfers between devices: 250 us -> 32.2 us
  Pallas kernels: 77.6 us -> 279 us
  local copies, waits for them, and re-layouts: 16.4 us -> 80.6 us
  blocking collectives: 46.9 us -> 0 us
  matrix products: 124 us -> 87.2 us
  other arithmetic: 22.4 us -> 11.9 us
    pallas_call x0 -> x1, Pallas kernels: none -> 201 us  [finish(): pl.pallas_call(functools.partial(finish_kernel, feat // 2), out_shape=(ja...]
    psum x1 -> x0, waiting for transfers between devices: 190 us -> none  [per_device(): late = lax.psum(grad_w_qkv, both)]
    psum x1 -> x0, blocking collectives: 46.9 us -> none  [per_device(): lax.psum((grad_b_out, grad_gain1, grad_shift1, grad_b_in, grad_b_back, gr...]
    dot_general x17 -> x14, matrix products: 124 us -> 87.2 us  [dot(): return lax.dot_general(a, b, dims, preferred_element_type=jnp.float32)]
    transpose x0 -> x4, local copies, waits for them, and re-layouts: none -> 32.2 us  [the longest x2 17.7 us: per_device(): full_in = grads[0].transpose(1, 0, 2).reshape(w_in.shape)]
    reduce_scatter x1 -> x0, waiting for transfers between devices: 30.1 us -> none  [per_device(): lax.psum_scatter(partial, 'seq', scatter_dimension=0, tiled=True)]
    unnamed x64 -> x52, local copies, waits for them, and re-layouts: 14.2 us -> 31.1 us
    convert_element_type x3 -> x2, other arithmetic: 15.6 us -> 2.85 us  [the longest x1 2.42 us: per_device(): grads = grads.astype(wide)]
  transfers between devices with their start and end apart: 3 -> 1, of which waited for: 3 -> 1; matrix products, arithmetic and copies ran while one was open for 9% -> 2% of each run, Pallas kernels for 0% -> 0%
where the time goes in v2:
time: 516 us; the launch traced here: 506 us
  Pallas kernels  279 us (54%)
  matrix products  87.2 us (17%)
  local copies, waits for them, and re-layouts  80.6 us (16%)
  waiting for transfers between devices  32.2 us (6%)
  between operations  15.5 us (3%)
  other arithmetic  11.9 us (2%)
    pallas_call x1, Pallas kernels, finish(): pl.pallas_call(functools.partial(finish_kernel, feat // 2), out_shape=(ja...  201 us
    dot_general x14, matrix products, dot(): return lax.dot_general(a, b, dims, preferred_element_type=jnp.float32)  87.2 us
    pallas_call x1, Pallas kernels, attend_back(): pl.pallas_call(functools.partial(attend_back_kernel, blocks), grid=(quads...  42.1 us
    pallas_call x1, Pallas kernels, attend(): pl.pallas_call(functools.partial(attend_kernel, blocks), grid=(quads,), o...  35.7 us
    all_gather x1, waiting for transfers between devices, per_device(): group_tokens = lax.all_gather(tokens, 'seq', axis=0, tiled=True)  31.5 us
    unnamed x52, local copies, waits for them, and re-layouts  31.1 us
    transpose x2, local copies, waits for them, and re-layouts, per_device(): full_in = grads[0].transpose(1, 0, 2).reshape(w_in.shape)  17.7 us
    transpose x2, local copies, waits for them, and re-layouts, per_device(): full_qkv = grads[2, :3].transpose(1, 0, 2).reshape(w_qkv.shape)  14.5 us
  transfers between devices with their start and end apart: 1, of which 1 were waited for; matrix products, arithmetic and copies ran while one was open for 2% of the time, Pallas kernels for 0%

profile of v2, /device:TPU:25, one launch (start us, length us, event | category | flops | bytes accessed | tf_op | source)
XLA Modules:
  0.0 506.1 jit_solution(18214672985777077046)
XLA Ops:
  13.3 3.7 fusion.15.q_ref
  17.0 31.5 %all-gather.2.cloned.1.call-done.tok_ref = bf16[3072,768]{1,0:T(8,128)(2,1)} async-done(((bf16[768,768]{1,0:T(8,128)(2,1)}), bf16[3072,768]{1,0:T(8,128)(2,1)}) %all-gather.2.cloned.1.call-update) | async-done | bytes 4718608 | tf_op jit(solution)/shard_map/all_gather | solution.py:664
  48.5 12.6 %convolution_convert_fusion.k_ref.v_ref = bf16[3072,1536]{1,0:T(8,128)(2,1)} fusion(bf16[3072,768]{1,0:T(8,128)(2,1)} %all-gather.2.cloned.1.call-done.tok_ref, bf16[768,2304]{1,0:T(8,128)(2,1)} %w_ref.1), kind=kOutput, calls=%fused_computation.1 | convolution fusion | flops 7252475904 | bytes 16515072 | tf_op jit(solution)/shard_map/dot_general | solution.py:24
  61.1 35.7 %attend.1 = (bf16[768,768]{1,0:T(8,128)(2,1)}, f32[3,16,256]{2,1,0:T(8,128)}) custom-call(s32[96]{0:T(128)} %min.12.ids_ref, s32[96]{0:T(128)} %reshape.257.lim_ref, s32[48]{0:T(128)} %reshape.242.glob_ref, bf16[768,768]{1,0:T(8,128)(2,1)} %fusion.15.q_ref, bf16[3072,1536]{1,0:T(8,128)(2,1)} %convolution_convert_fusion.k_ref.v_ref, ...), custom_call_target="tpu_custom_call" | custom-call | tf_op jit(solution)/shard_map/attend/pallas_call | solution.py:121
  96.9 2.5 fusion.39
  100.7 27.0 %multiply_convert_fusion = (bf16[768,3072]{1,0:T(8,128)(2,1)S(1)}, f32[768,3072]{1,0:T(8,128)}, f32[768,3072]{1,0:T(8,128)}) fusion(f32[3072]{0:T(1024)S(1)} %copy-done.16, bf16[768,768]{1,0:T(8,128)(2,1)S(1)} %fusion.14, bf16[768,3072]{1,0:T(8,128)(2,1)} %param.25), kind=kOutput, calls=%fused_computation.6 | convolution fusion | flops 3779592192 | bytes 29503488 | tf_op jit(solution)/shard_map/dot_general | solution.py:24
  127.8 4.1 fusion.40
  136.2 5.6 %convolution_convert_fusion.1 = bf16[3072,768]{1,0:T(8,128)(2,1)} fusion(bf16[768,3072]{1,0:T(8,128)(2,1)S(1)} %get-tuple-element.73, f32[768,768]{1,0:T(8,128)S(1)} %get-tuple-element.70), kind=kOutput, calls=%fused_computation.21 | convolution fusion | flops 3626827776 | bytes 11796480 | tf_op jit(solution)/shard_map/dot_general | solution.py:24
  141.9 12.9 %convert_reduce_fusion = (f32[3072]{0:T(1024)}, bf16[768,3072]{1,0:T(8,128)(2,1)}) fusion(f32[768,3072]{1,0:T(8,128)} %get-tuple-element.74, bf16[3072,768]{1,0:T(8,128)(2,1)S(1)} %bitcast.54, f32[768,768]{1,0:T(8,128)S(1)} %get-tuple-element.70, f32[768,3072]{1,0:T(8,128)} %get-tuple-element.86, f32[3072]{0:T(1024)S(1)} %copy-done.16), kind=kOutput, calls=%fused_computation.4 | convolution fusion | flops 3664573440 | bytes 30695424 | tf_op jit(solution)/shard_map/dot_general | solution.py:24
  154.8 3.6 fusion.19
  164.8 4.5 multiply_reduce_fusion
  172.4 2.2 convolution_convert_fusion.3.w_out_ref
  176.1 42.1 %attend_back.1 = (bf16[768,768]{1,0:T(8,128)(2,1)}, bf16[3072,768]{1,0:T(8,128)(2,1)}, bf16[3072,768]{1,0:T(8,128)(2,1)}) custom-call(s32[96]{0:T(128)} %min.12.ids_ref, s32[96]{0:T(128)} %reshape.257.lim_ref, s32[48]{0:T(128)} %reshape.242.glob_ref, bf16[768,768]{1,0:T(8,128)(2,1)} %fusion.15.q_ref, bf16[3072,1536]{1,0:T(8,128)(2,1)} %convolution_convert_fusion.k_ref.v_ref, ...), custom_call_target="tpu_custom_call" | custom-call | tf_op jit(solution)/shard_map/attend_back/pallas_call | solution.py:238
  218.3 2.5 pad_maximum_fusion.w_in_ref
  220.8 200.9 %finish.1 = (bf16[3,4,768,768]{3,2,1,0:T(8,128)(2,1)}, bf16[768,768]{1,0:T(8,128)(2,1)}, f32[16,768]{1,0:T(8,128)}) custom-call(bf16[4,768,768]{2,1,0:T(8,128)(2,1)} %pad_maximum_fusion.w_in_ref, bf16[4,768,768]{2,1,0:T(8,128)(2,1)} %bitcast.50, bf16[768,768]{1,0:T(8,128)(2,1)} %convolution_convert_fusion.3.w_out_ref, f32[16,768]{1,0:T(8,128)} %pad.4.small_ref, ...), custom_call_target="tpu_custom_call" | custom-call | tf_op jit(solution)/shard_map/finish/pallas_call | solution.py:569
  424.2 8.1 %slice.75 = f32[1,4,768,768]{3,2,1,0:T(8,128)} slice(bf16[3,4,768,768]{3,2,1,0:T(8,128)(2,1)} %get-tuple-element.27), slice={[1:2], [0:4], [0:768], [0:768]} | slice | bytes 18874368 | tf_op jit(solution)/shard_map/slice | solution.py:723
  434.0 2.4 convert_element_type.102
  436.5 9.3 %copy-done.1 = f32[3,4,768,768]{3,2,1,0:T(8,128)} copy-done((f32[3,4,768,768]{3,2,1,0:T(8,128)}, f32[3,4,768,768]{3,2,1,0:T(8,128)S(1)}, u32[]{:S(2)}) %copy-start.1) | copy-done | bytes 28311576
  447.4 6.4 %slice_bitcast_fusion.1 = f32[768,3,768]{2,0,1:T(8,128)} fusion(f32[3,4,768,768]{3,2,1,0:T(8,128)} %copy-done.1), kind=kLoop, calls=%fused_computation.20 | loop fusion | bytes 14155776 | tf_op jit(solution)/shard_map/transpose | solution.py:724
  453.8 8.0 %slice_bitcast_fusion = f32[768,4,768]{2,0,1:T(8,128)} fusion(f32[3,4,768,768]{3,2,1,0:T(8,128)} %copy-done.1), kind=kLoop, calls=%fused_computation.3 | loop fusion | bytes 18874368 | tf_op jit(solution)/shard_map/transpose | solution.py:722
  462.4 9.7 %copy.46 = f32[768,4,768]{0,2,1:T(8,128)} copy(f32[768,4,768]{2,0,1:T(8,128)} %slice_bitcast_fusion) | data formatting | bytes 18874368 | tf_op jit(solution)/shard_map/transpose | solution.py:722
  472.1 9.6 %copy.48 = f32[768,3072]{1,0:T(8,128)} copy(f32[768,3072]{0,1:T(8,128)} %bitcast.47) | data formatting | bytes 18874368
  481.7 8.1 %copy.45 = f32[768,3,768]{0,2,1:T(8,128)} copy(f32[768,3,768]{2,0,1:T(8,128)} %slice_bitcast_fusion.1) | data formatting | bytes 14155776 | tf_op jit(solution)/shard_map/transpose | solution.py:724
  489.8 8.1 %copy.47 = f32[768,2304]{1,0:T(8,128)} copy(f32[768,2304]{0,1:T(8,128)} %bitcast.48) | data formatting | bytes 14155776
  (105 shorter events, 29.6 us)
Async XLA Ops:
  7.2 89.7 %copy-start = (bf16[768,768]{1,0:T(8,128)(2,1)S(1)}, bf16[768,768]{1,0:T(8,128)(2,1)}, u32[]{:S(2)}) copy-start(bf16[768,768]{1,0:T(8,128)(2,1)} %param.21) | copy-start | bytes 3538948
  7.2 41.3 %all-gather.2.cloned.1.call-start = ((), (), s32[]{:S(2)}) async-start(), calls=%async_computation | async-start | bytes 5898240 | tf_op jit(solution)/shard_map/all_gather | solution.py:664
  61.1 35.8 %copy-start.10 = (bf16[768,768]{1,0:T(8,128)(2,1)S(1)}, bf16[768,768]{1,0:T(8,128)(2,1)}, u32[]{:S(2)}) copy-start(bf16[768,768]{1,0:T(8,128)(2,1)} %param.16) | copy-start | bytes 3538948
  61.1 35.8 %copy-start.17 = (f32[768]{0:T(1024)S(1)}, f32[768]{0:T(1024)}, u32[]{:S(2)}) copy-start(f32[768]{0:T(1024)} %param.22) | copy-start | bytes 9220
  99.4 0.7 copy-start.14
  99.4 28.3 %slice-start = ((s8[4718592]{0:T(1024)(128)(4,1)}), s8[4194304]{0:T(1024)(128)(4,1)S(1)}, s32[]{:S(2)}) async-start(s8[4718592]{0:T(1024)(128)(4,1)} %bitcast.53), calls=%async_computation.1 | async-start | bytes 8388608
  99.8 0.9 copy-start.16
  100.7 27.0 %slice-start.1 = ((s8[4718592]{0:T(1024)(128)(4,1)}), s8[524288]{0:T(1024)(128)(4,1)S(1)}, s32[]{:S(2)}) async-start(s8[4718592]{0:T(1024)(128)(4,1)} %bitcast.53), calls=%async_computation.2 | async-start | bytes 1048576
  100.7 27.0 %copy-start.18 = (f32[768]{0:T(1024)S(1)}, f32[768]{0:T(1024)}, u32[]{:S(2)}) copy-start(f32[768]{0:T(1024)} %param.28) | copy-start | bytes 9220
  131.9 1.3 copy-start.4
  131.9 1.3 copy-start.13
  132.3 2.0 copy-start.15
  154.8 3.6 copy-start.19
  160.5 4.4 slice-start.2
  162.7 2.2 slice-start.3
  170.2 2.2 copy-start.3
  170.2 2.1 copy-start.5
  176.1 42.1 %copy-start.6 = (bf16[1,768,768]{2,1,0:T(8,128)(2,1)S(1)}, bf16[1,768,768]{2,1,0:T(8,128)(2,1)}, u32[]{:S(2)}) copy-start(bf16[1,768,768]{2,1,0:T(8,128)(2,1)} %fusion.19) | copy-start | bytes 3538948
  176.1 42.1 %copy-start.7 = (bf16[1,768,768]{2,1,0:T(8,128)(2,1)S(1)}, bf16[1,768,768]{2,1,0:T(8,128)(2,1)}, u32[]{:S(2)}) copy-start(bf16[1,768,768]{2,1,0:T(8,128)(2,1)} %fusion.18) | copy-start | bytes 3538948
  176.1 42.1 %copy-start.8 = (bf16[1,768,768]{2,1,0:T(8,128)(2,1)S(1)}, bf16[1,768,768]{2,1,0:T(8,128)(2,1)}, u32[]{:S(2)}) copy-start(bf16[1,768,768]{2,1,0:T(8,128)(2,1)} %fusion.17) | copy-start | bytes 3538948
  176.1 42.1 %copy-start.9 = (bf16[1,768,768]{2,1,0:T(8,128)(2,1)S(1)}, bf16[1,768,768]{2,1,0:T(8,128)(2,1)}, u32[]{:S(2)}) copy-start(bf16[1,768,768]{2,1,0:T(8,128)(2,1)} %fusion.16) | copy-start | bytes 3538948
  424.2 9.8 %copy-start.2 = (bf16[3,4,768,768]{3,2,1,0:T(8,128)(2,1)S(1)}, bf16[3,4,768,768]{3,2,1,0:T(8,128)(2,1)}, u32[]{:S(2)}) copy-start(bf16[3,4,768,768]{3,2,1,0:T(8,128)(2,1)} %get-tuple-element.27) | copy-start | bytes 42467332
  436.5 9.4 %copy-start.1 = (f32[3,4,768,768]{3,2,1,0:T(8,128)}, f32[3,4,768,768]{3,2,1,0:T(8,128)S(1)}, u32[]{:S(2)}) copy-start(f32[3,4,768,768]{3,2,1,0:T(8,128)S(1)} %convert_element_type.102) | copy-start | bytes 84934656
  489.8 8.1 %copy-start.11 = (bf16[768,768]{1,0:T(8,128)(2,1)S(1)}, bf16[768,768]{1,0:T(8,128)(2,1)}, u32[]{:S(2)}) copy-start(bf16[768,768]{1,0:T(8,128)(2,1)} %get-tuple-element.112) | copy-start | bytes 3538948
  (1 other events, 0.7 us)
Sparse Core Ops, SparseCore 0:
  9.6 38.8 all-gather.1
